TPU v7x, 1024 devices: a whole 4x4x32 slice. The times are simulated.
1024 devices in a mesh: row: 16 (over x_hi, y, core), col: 64 (over x_lo, z).
Axes of the slice: x: 4 (x_hi: 2, x_lo: 2; x = x_hi * 2 + x_lo), y: 4, z: 32, core: 2. Of those that a mesh axis runs over, the one named last changes fastest.
Arguments:
- inputs: bfloat16 [1024, 6144], P('col', 'row'), may hold values from -6 to 6
- out_grad: bfloat16 [1024, 6144], P('col', 'row'), may hold values from -6 to 6
- w_first: bfloat16 [6144, 24576], P('row', 'col'), may hold values from -0.078125 to 0.078125
- w_second: bfloat16 [24576, 6144], P('col', 'row'), may hold values from -0.0390625 to 0.0390625
Outputs:
- d_input: bfloat16 [1024, 6144], P('col', 'row')
- grad_first: float32 [6144, 24576], P('row', 'col')
- grad_second: float32 [24576, 6144], P('col', 'row')
All inputs are finite; a program needn't handle non-finite values.
Results may differ from a plain program's by a relative error of at most 0.0049.
Values may be sent and summed in bfloat16 or wider, within the bound.
No kernel may reach another device: no remote copies, remote signals or barrier semaphores. Data moves between devices by JAX's collectives and lax.ppermute only.
A program may use at most 32 MiB of HBM per device.

v0:
```python
import math

import jax
import jax.numpy as jnp
from jax import lax
from jax.sharding import PartitionSpec as P


def gelu_pair(pre):
    cdf = 0.5 * (1.0 + jax.scipy.special.erf(pre / math.sqrt(2.0)))
    dens = jnp.exp(-0.5 * pre * pre) / math.sqrt(2.0 * math.pi)
    return (pre * cdf, cdf + pre * dens)


def activate(pre, back):
    value, slope = gelu_pair(pre)
    return (value.astype(jnp.bfloat16), (back * slope).astype(jnp.bfloat16))


def local(inputs, out_grad, w_first, w_second):
    gathered_in, gathered_grad = (
        lax.all_gather(inputs, "col", axis=0, tiled=True),
        lax.all_gather(out_grad, "col", axis=0, tiled=True),
    )
    pre_part = jnp.dot(gathered_in, w_first, preferred_element_type=jnp.float32)
    back_part = lax.dot_general(
        gathered_grad, w_second, (((1,), (1,)), ((), ())), preferred_element_type=jnp.float32
    )
    pre_share, back_share = (
        lax.psum_scatter(pre_part, "row", scatter_dimension=0, tiled=True),
        lax.psum_scatter(back_part, "row", scatter_dimension=0, tiled=True),
    )
    act_share, dpre_share = activate(pre_share, back_share)
    act_all, dpre_all = (
        lax.all_gather(act_share, "row", axis=0, tiled=True),
        lax.all_gather(dpre_share, "row", axis=0, tiled=True),
    )
    grad_second = lax.dot_general(
        act_all, gathered_grad, (((0,), (0,)), ((), ())), preferred_element_type=jnp.float32
    )
    grad_first = lax.dot_general(
        gathered_in, dpre_all, (((0,), (0,)), ((), ())), preferred_element_type=jnp.float32
    )
    d_input = lax.psum_scatter(
        lax.dot_general(
            dpre_all, w_first, (((1,), (1,)), ((), ())), preferred_element_type=jnp.float32
        ),
        "col",
        scatter_dimension=0,
        tiled=True,
    )
    return (d_input.astype(jnp.bfloat16), grad_first, grad_second)


def solution(mesh):
    placed = (P("col", "row"), P("col", "row"), P("row", "col"), P("col", "row"))
    return jax.shard_map(
        local,
        mesh=mesh,
        in_specs=placed,
        out_specs=(P("col", "row"), P("row", "col"), P("col", "row")),
        check_vma=False,
    )
```

profile of v0, /device:TPU:24, one launch (start us, length us, event | category | flops | bytes accessed | tf_op | source)
XLA Modules:
  0.0 681.1 jit_solution(14330197166761106321)
XLA Ops:
  7.2 0.0 copy-start
  7.2 0.0 reduce-scatter.4.cloned.1.call-start
  7.2 138.4 %all_gather.12 = bf16[1024,384]{1,0:T(8,128)(2,1)S(1)} all-gather(bf16[16,384]{1,0:T(8,128)(2,1)} %param.5), channel_id=1, replica_groups=mesh['row'=16,'col'=64] {'col'}, dimensions={0}, use_global_device_ids=true | all-gather | bytes 798720 | tf_op jit(solution)/shard_map/all_gather | solution.py:23
  145.6 0.0 copy-start.1
  145.7 2.8 fusion.6
  148.4 0.0 reduce-scatter.4.cloned.1.call-update
  148.5 0.0 reduce-scatter.6.cloned.1.call-start
  148.5 0.0 copy-done.1
  148.5 120.8 %all_gather.13 = bf16[1024,384]{1,0:T(8,128)(2,1)S(1)} all-gather(bf16[16,384]{1,0:T(8,128)(2,1)S(1)} %copy-done.1), channel_id=1, replica_groups=mesh['row'=16,'col'=64] {'col'}, dimensions={0}, use_global_device_ids=true | all-gather | bytes 798720 | tf_op jit(solution)/shard_map/all_gather | solution.py:22
  269.3 0.0 copy-done
  269.3 1.8 fusion.7
  271.1 0.0 reduce-scatter.6.cloned.1.call-update
  271.1 0.0 reduce-scatter.8.cloned.1.call-start
  271.2 0.0 reduce-scatter.4.cloned.1.call-done
  271.2 109.7 %reduce-scatter.6.cloned.1.call-done = f32[64,384]{1,0:T(8,128)} async-done(((f32[1024,384]{1,0:T(8,128)}), f32[64,384]{1,0:T(8,128)}) %reduce-scatter.6.cloned.1.call-update) | async-done | bytes 98320 | tf_op jit(solution)/shard_map/reduce_scatter | solution.py:30
  380.9 1.0 multiply_convert_fusion
  381.9 20.4 %all_gather.14 = bf16[1024,384]{1,0:T(8,128)(2,1)S(1)} all-gather(bf16[64,384]{1,0:T(8,128)(2,1)S(1)} %get-tuple-element.7), channel_id=1, replica_groups=mesh['row'=16,'col'=64] {'row'}, dimensions={0}, use_global_device_ids=true | all-gather | bytes 835584 | tf_op jit(solution)/shard_map/all_gather | solution.py:36
  402.2 1.8 fusion.8
  404.0 0.0 reduce-scatter.8.cloned.1.call-update
  404.1 0.6 convolution_bitcast_fusion
  404.7 1.1 copy.7
  405.7 23.8 %all_gather.15 = bf16[1024,384]{1,0:T(8,128)(2,1)S(1)} all-gather(bf16[64,384]{1,0:T(8,128)(2,1)S(1)} %get-tuple-element.6), channel_id=1, replica_groups=mesh['row'=16,'col'=64] {'row'}, dimensions={0}, use_global_device_ids=true | all-gather | bytes 835584 | tf_op jit(solution)/shard_map/all_gather | solution.py:35
  429.5 1.4 fusion.9
  430.9 242.3 %reduce-scatter.8.cloned.1.call-done = f32[16,384]{1,0:T(8,128)} async-done(((f32[1024,384]{1,0:T(8,128)}), f32[16,384]{1,0:T(8,128)}) %reduce-scatter.8.cloned.1.call-update) | async-done | bytes 24592 | tf_op jit(solution)/shard_map/reduce_scatter | solution.py:44
  673.2 1.3 convert_element_type.10
Async XLA Ops:
  7.2 262.1 %copy-start = (bf16[384,384]{1,0:T(8,128)(2,1)S(1)}, bf16[384,384]{1,0:T(8,128)(2,1)}, u32[]{:S(2)}) copy-start(bf16[384,384]{1,0:T(8,128)(2,1)} %param.6) | copy-start | bytes 884740
  7.2 264.0 %reduce-scatter.4.cloned.1.call-start = ((), (), s32[]{:S(2)}) async-start(), calls=%async_computation.3 | async-start | bytes 1671168 | tf_op jit(solution)/shard_map/reduce_scatter | solution.py:31
  145.6 2.9 copy-start.1
  148.5 232.4 %reduce-scatter.6.cloned.1.call-start = ((), (), s32[]{:S(2)}) async-start(), calls=%async_computation.4 | async-start | bytes 1671168 | tf_op jit(solution)/shard_map/reduce_scatter | solution.py:30
  271.1 402.1 %reduce-scatter.8.cloned.1.call-start = ((), (), s32[]{:S(2)}) async-start(), calls=%async_computation.5 | async-start | bytes 1597440 | tf_op jit(solution)/shard_map/reduce_scatter | solution.py:44
Sparse Core Ops, SparseCore 0:
  148.6 103.0 reduce-scatter.3
  271.2 109.5 reduce-scatter.5
  404.2 268.9 reduce-scatter.7
where the time goes:
time: 682 us; the launch traced here: 681 us
  waiting for transfers between devices  352 us (52%)
  blocking collectives  303 us (44%)
  between operations  13.8 us (2%)
  matrix products  8.38 us (1%)
    reduce_scatter x1, waiting for transfers between devices, local(): lax.psum_scatter(lax.dot_general(dpre_all, w_first, (((1,), (1,)), ((), (...  242 us
    all_gather x1, blocking collectives, local(): lax.all_gather(out_grad, 'col', axis=0, tiled=True)  138 us
    all_gather x1, blocking collectives, local(): lax.all_gather(inputs, 'col', axis=0, tiled=True)  121 us
    reduce_scatter x1, waiting for transfers between devices, local(): lax.psum_scatter(pre_part, 'row', scatter_dimension=0, tiled=True)  110 us
    all_gather x1, blocking collectives, local(): lax.all_gather(act_share, 'row', axis=0, tiled=True)  23.8 us
    all_gather x1, blocking collectives, local(): lax.all_gather(dpre_share, 'row', axis=0, tiled=True)  20.4 us
  transfers between devices with their start and end apart: 3, of which 2 were waited for; matrix products, arithmetic and copies ran while one was open for 1% of the time, Pallas kernels for 0%

commit v1 on v0

v1 whole, which is shorter than its diff:
```python
import math

import jax
import jax.numpy as jnp
from jax import lax
from jax.sharding import Mesh, PartitionSpec as P

ROW = ("xh", "y", "core")
NEAR = ("xl", "zl")
FAR = ("zh",)
F32 = jnp.float32
BF16 = jnp.bfloat16


def gelu_pair(pre):
    cdf = 0.5 * (1.0 + jax.scipy.special.erf(pre / math.sqrt(2.0)))
    dens = jnp.exp(-0.5 * pre * pre) / math.sqrt(2.0 * math.pi)
    return (pre * cdf, cdf + pre * dens)


def exchange(blocks, axes):
    return lax.all_to_all(blocks, axes, 0, 0, tiled=False)


def spread(block, axes, size):
    return exchange(jnp.broadcast_to(block[None], (size,) + block.shape), axes)


def local(inputs, out_grad, w_first, w_second):
    rows, width = inputs.shape
    pair = jnp.stack([inputs, out_grad])
    far = spread(pair, FAR, 8)
    far = far.transpose(1, 0, 2, 3).reshape(2, 8 * rows, width)
    near = spread(far, NEAR, 8)
    tokens = 64 * rows
    all_in = near[:, 0].reshape(tokens, width)
    all_grad = near[:, 1].reshape(tokens, width)
    pre_part = jnp.dot(all_in, w_first, preferred_element_type=F32)
    back_part = lax.dot_general(
        all_grad, w_second, (((1,), (1,)), ((), ())), preferred_element_type=F32
    )
    hidden = pre_part.shape[1]
    parts = jnp.concatenate([pre_part.astype(BF16), back_part.astype(BF16)], axis=1)
    parts = exchange(parts.reshape(16, tokens // 16, 2 * hidden), ROW)
    sums = jnp.sum(parts.astype(F32), axis=0)
    value, slope = gelu_pair(sums[:, :hidden])
    both = jnp.concatenate(
        [value.astype(BF16), (sums[:, hidden:] * slope).astype(BF16)], axis=1
    )
    both = spread(both, ROW, 16).reshape(tokens, 2 * hidden)
    act, d_pre = both[:, :hidden], both[:, hidden:]
    terms = lax.dot_general(
        d_pre, w_first, (((1,), (1,)), ((), ())), preferred_element_type=F32
    ).astype(BF16)
    terms = exchange(terms.reshape(8, 8 * rows, width), NEAR)
    terms = jnp.sum(terms.astype(F32), axis=0).astype(BF16)
    terms = exchange(terms.reshape(8, rows, width), FAR)
    d_input = jnp.sum(terms.astype(F32), axis=0).astype(BF16)
    grad_second = lax.dot_general(
        act, all_grad, (((0,), (0,)), ((), ())), preferred_element_type=F32
    )
    grad_first = lax.dot_general(
        all_in, d_pre, (((0,), (0,)), ((), ())), preferred_element_type=F32
    )
    return (d_input, grad_first, grad_second)


def solution(mesh):
    fine = Mesh(mesh.devices.reshape(2, 4, 2, 2, 8, 4), ("xh", "y", "core", "xl", "zh", "zl"))
    row, col = ROW, ("xl", "zh", "zl")
    placed = (P(col, row), P(col, row), P(row, col), P(col, row))
    return jax.shard_map(
        local,
        mesh=fine,
        in_specs=placed,
        out_specs=(P(col, row), P(row, col), P(col, row)),
        check_vma=False,
    )
```

time: 682 us -> 222 us (0.33)
  the two profiles are of different devices: /device:TPU:24 before, /device:TPU:1 now
where the time goes in v1:
time: 222 us; the launch traced here: 220 us
  blocking collectives  184 us (83%)
  waiting for transfers between devices  21.5 us (10%)
  starting transfers between devices  4.85 us (2%)
  matrix products  4.69 us (2%)
  other arithmetic  2.54 us (1%)
    all_to_all x5, blocking collectives, exchange(): return lax.all_to_all(blocks, axes, 0, 0, tiled=False)  184 us
    all_to_all x1, waiting for transfers between devices, exchange(): return lax.all_to_all(blocks, axes, 0, 0, tiled=False)  21.5 us
    all_to_all x1, starting transfers between devices, exchange(): return lax.all_to_all(blocks, axes, 0, 0, tiled=False)  4.85 us
  transfers between devices with their start and end apart: 1, of which 1 were waited for; matrix products, arithmetic and copies ran while one was open for 1% of the time, Pallas kernels for 0%

profile of v1, /device:TPU:1, one launch (start us, length us, event | category | flops | bytes accessed | tf_op | source)
XLA Modules:
  0.0 220.1 jit_solution(7171347720099258051)
XLA Ops:
  0.6 0.0 copy-start
  0.6 0.8 pad_maximum_fusion.2
  1.4 56.1 %all_to_all.30 = bf16[8,2,16,384]{3,2,1,0:T(8,128)(2,1)S(1)} all-to-all(bf16[8,2,16,384]{3,2,1,0:T(8,128)(2,1)S(1)} %broadcast_in_dim.8), channel_id=1, replica_groups=mesh['xh'=2,'y'=4,'core'=2,'xl'=2,'zh'=8,'zl'=4] {'zh'}, dimensions={0} | all-to-all | bytes 393216 | tf_op jit(solution)/shard_map/all_to_all | solution.py:22
  57.6 0.2 broadcast_in_dim.10
  57.8 47.4 %all_to_all.31 = bf16[8,2,128,384]{3,2,1,0:T(8,128)(2,1)S(1)} all-to-all(bf16[8,2,128,384]{3,2,1,0:T(8,128)(2,1)S(1)} %broadcast_in_dim.10), channel_id=1, replica_groups=mesh['xh'=2,'y'=4,'core'=2,'xl'=2,'zh'=8,'zl'=4] {'xl','zl'}, dimensions={0} | all-to-all | bytes 3145728 | tf_op jit(solution)/shard_map/all_to_all | solution.py:22
  105.2 0.2 fusion.11
  105.4 0.0 copy-start.1
  105.4 0.0 copy-start.3
  105.4 0.8 copy-done.5
  106.2 0.6 convolution_convert_fusion.1
  106.8 0.0 copy-done.1
  106.8 0.0 copy-done.3
  106.8 0.0 copy-done
  106.8 0.6 convolution_convert_fusion.2
  107.4 0.1 pad_maximum_fusion
  107.5 0.7 copy.11
  108.3 31.4 %all_to_all.32 = bf16[16,64,768]{2,1,0:T(8,128)(2,1)S(1)} all-to-all(bf16[16,64,768]{2,1,0:T(8,128)(2,1)S(1)} %bitcast.18), channel_id=1, replica_groups=mesh['xh'=2,'y'=4,'core'=2,'xl'=2,'zh'=8,'zl'=4] {'xh','y','core'}, dimensions={0} | all-to-all | bytes 3145728 | tf_op jit(solution)/shard_map/all_to_all | solution.py:22
  139.7 0.2 convert_reduce_fusion
  139.9 0.1 multiply_convert_fusion
  140.0 0.1 broadcast_in_dim.22
  140.2 26.2 %all_to_all.33 = bf16[16,64,768]{2,1,0:T(8,128)(2,1)S(1)} all-to-all(bf16[16,64,768]{2,1,0:T(8,128)(2,1)S(1)} %broadcast_in_dim.22), channel_id=1, replica_groups=mesh['xh'=2,'y'=4,'core'=2,'xl'=2,'zh'=8,'zl'=4] {'xh','y','core'}, dimensions={0} | all-to-all | bytes 3145728 | tf_op jit(solution)/shard_map/all_to_all | solution.py:22
  166.4 0.6 convolution_convert_fusion
  167.0 0.0 copy-start.4
  167.0 22.4 %all_to_all.34 = bf16[8,128,384]{2,1,0:T(8,128)(2,1)S(1)} all-to-all(bf16[8,128,384]{2,1,0:T(8,128)(2,1)S(1)} %bitcast.27), channel_id=1, replica_groups=mesh['xh'=2,'y'=4,'core'=2,'xl'=2,'zh'=8,'zl'=4] {'xl','zl'}, dimensions={0} | all-to-all | bytes 1572864 | tf_op jit(solution)/shard_map/all_to_all | solution.py:22
  189.5 0.7 reduce_sum.34
  190.2 4.9 %all-to-all-start.5 = ((bf16[8,16,384]{2,1,0:T(8,128)(2,1)}), bf16[8,16,384]{2,1,0:T(8,128)(2,1)S(1)}, u32[]{:S(2)}, u32[]{:S(2)}) async-start(bf16[8,16,384]{2,1,0:T(8,128)(2,1)} %bitcast.28), calls=%async_computation.5 | async-start | bytes 196608 | tf_op jit(solution)/shard_map/all_to_all | solution.py:22
  195.1 0.0 copy-done.4
  195.1 1.4 fusion.2
  196.5 0.0 copy-done.2
  196.5 1.4 fusion
  197.9 21.5 %all-to-all-done.5 = bf16[8,16,384]{2,1,0:T(8,128)(2,1)S(1)} async-done(((bf16[8,16,384]{2,1,0:T(8,128)(2,1)}), bf16[8,16,384]{2,1,0:T(8,128)(2,1)S(1)}, u32[]{:S(2)}, u32[]{:S(2)}) %all-to-all-start.5) | async-done | bytes 98336 | tf_op jit(solution)/shard_map/all_to_all | solution.py:22
  219.4 0.6 reduce_sum.35
  (5 shorter events, 0.1 us)
Async XLA Ops:
  0.6 106.2 %copy-start = (bf16[384,384]{1,0:T(8,128)(2,1)S(1)}, bf16[384,384]{1,0:T(8,128)(2,1)}, u32[]{:S(2)}) copy-start(bf16[384,384]{1,0:T(8,128)(2,1)} %param.6) | copy-start | bytes 884740
  105.2 1.0 copy-start.5
  105.4 1.4 copy-start.1
  105.4 1.4 copy-start.3
  167.0 28.0 %copy-start.4 = (bf16[8,1,128,384]{3,2,1,0:T(8,128)(2,1)S(1)}, bf16[8,1,128,384]{3,2,1,0:T(8,128)(2,1)}, u32[]{:S(2)}) copy-start(bf16[8,1,128,384]{3,2,1,0:T(8,128)(2,1)} %copy-done.3) | copy-start | bytes 2359300
  190.2 6.3 %copy-start.2 = (bf16[8,1,128,384]{3,2,1,0:T(8,128)(2,1)S(1)}, bf16[8,1,128,384]{3,2,1,0:T(8,128)(2,1)}, u32[]{:S(2)}) copy-start(bf16[8,1,128,384]{3,2,1,0:T(8,128)(2,1)} %copy-done.1) | copy-start | bytes 2359300
  190.2 29.2 %all-to-all-start.5 = ((bf16[8,16,384]{2,1,0:T(8,128)(2,1)}), bf16[8,16,384]{2,1,0:T(8,128)(2,1)S(1)}, u32[]{:S(2)}, u32[]{:S(2)}) async-start(bf16[8,16,384]{2,1,0:T(8,128)(2,1)} %bitcast.28), calls=%async_computation.5 | async-start | bytes 196608 | tf_op jit(solution)/shard_map/all_to_all | solution.py:22

commit v2 on v1

v2 whole, which is shorter than its diff:
```python
import math

import jax
import jax.numpy as jnp
from jax import lax
from jax.sharding import Mesh, PartitionSpec as P

QUAD = ("core", "xl")
PLANE = ("xh", "y")
FAR = ("core", "zh")
NEAR = ("zl",)
F32 = jnp.float32
BF16 = jnp.bfloat16


def gelu_pair(pre):
    cdf = 0.5 * (1.0 + jax.scipy.special.erf(pre / math.sqrt(2.0)))
    dens = jnp.exp(-0.5 * pre * pre) / math.sqrt(2.0 * math.pi)
    return (pre * cdf, cdf + pre * dens)


def exchange(blocks, axes):
    return lax.all_to_all(blocks, axes, 0, 0, tiled=False)


def flip(block, slab, column):
    return lax.ppermute(block, QUAD, [(i, i ^ (2 * slab + column)) for i in range(4)])


def dot(a, b, ca, cb):
    return lax.dot_general(a, b, (((ca,), (cb,)), ((), ())), preferred_element_type=F32)


def local(inputs, out_grad, w_first, w_second):
    rows, width = inputs.shape
    half = rows // 2
    core = lax.axis_index("core")

    packed = jnp.concatenate([w_first, w_second])
    held = [[packed, flip(packed, 0, 1)], [flip(packed, 1, 0), flip(packed, 1, 1)]]
    first = [[held[s][c][:width] for c in range(2)] for s in range(2)]
    second = [[held[s][c][width:] for c in range(2)] for s in range(2)]

    pair = jnp.stack([inputs, out_grad]).reshape(2, 2, half, width).transpose(1, 0, 2, 3)
    pair = jnp.broadcast_to(pair[:, None], (2, 8, 2, half, width))
    far = exchange(pair.reshape(16, 2, half, width), FAR).reshape(2, 8, 2, half, width)
    far = far.transpose(2, 0, 1, 3, 4).reshape(2, 2, 8 * half, width)
    own_in, own_grad = [jnp.where(core == 0, f[0], f[1]) for f in far]
    other_in, other_grad = [jnp.where(core == 0, f[1], f[0]) for f in far]
    far = jnp.concatenate([own_in, other_in, own_grad, other_grad], axis=1)
    near = lax.all_gather(far, NEAR, axis=0, tiled=True)
    tokens = near.shape[0]
    x = [near[:, s * width : (s + 1) * width] for s in range(2)]
    g = [near[:, (2 + s) * width : (3 + s) * width] for s in range(2)]

    pre = [dot(x[0], first[0][c], 1, 0) + dot(x[1], first[1][c], 1, 0) for c in range(2)]
    back = [dot(g[0], second[0][c], 1, 1) + dot(g[1], second[1][c], 1, 1) for c in range(2)]
    parts = jnp.concatenate([p.astype(BF16) for p in pre + back], axis=1)
    parts = exchange(parts.reshape(8, tokens // 8, 4 * width), PLANE)
    sums = jnp.sum(parts.astype(F32), axis=0)
    value, slope = gelu_pair(sums[:, : 2 * width])
    both = jnp.concatenate(
        [value.astype(BF16), (sums[:, 2 * width :] * slope).astype(BF16)], axis=1
    )
    both = exchange(jnp.broadcast_to(both[None], (8,) + both.shape), PLANE)
    both = both.reshape(tokens, 4 * width)
    act = [both[:, c * width : (c + 1) * width] for c in range(2)]
    d_pre = [both[:, (2 + c) * width : (3 + c) * width] for c in range(2)]

    terms = [dot(d_pre[0], first[s][0], 1, 1) + dot(d_pre[1], first[s][1], 1, 1) for s in range(2)]
    terms = jnp.concatenate([t.astype(BF16) for t in terms], axis=1)
    terms = exchange(terms.reshape(4, tokens // 4, 2 * width), NEAR)
    terms = jnp.sum(terms.astype(F32), axis=0).astype(BF16)
    own, other = terms[:, :width], terms[:, width:]
    terms = jnp.stack([jnp.where(core == 0, own, other), jnp.where(core == 0, other, own)])
    terms = exchange(terms.reshape(16, half, width), FAR).reshape(2, 8, half, width)
    d_input = jnp.sum(terms.astype(F32), axis=1).astype(BF16).reshape(rows, width)

    def grads(s, c):
        return (dot(x[s], d_pre[c], 0, 0), dot(act[c], g[s], 0, 0))

    grad_first, grad_second = grads(0, 0)
    for s, c in ((1, 0), (0, 1), (1, 1)):
        sent = jnp.concatenate([t.astype(BF16) for t in grads(s, c)])
        came = flip(sent, s, c).astype(F32)
        grad_first = grad_first + came[:width]
        grad_second = grad_second + came[width:]
    return (d_input, grad_first, grad_second)


def solution(mesh):
    fine = Mesh(mesh.devices.reshape(2, 4, 2, 2, 8, 4), ("xh", "y", "core", "xl", "zh", "zl"))
    row, col = ("xh", "y", "core"), ("xl", "zh", "zl")
    placed = (P(col, row), P(col, row), P(row, col), P(col, row))
    return jax.shard_map(
        local,
        mesh=fine,
        in_specs=placed,
        out_specs=(P(col, row), P(row, col), P(col, row)),
        check_vma=False,
    )
```

time: 222 us -> 175 us (0.79)
  blocking collectives: 184 us -> 44 us
  starting transfers between devices: 4.85 us -> 72.6 us
  waiting for transfers between devices: 21.5 us -> 37.6 us
  other arithmetic: 2.54 us -> 7.13 us
  matrix products: 4.69 us -> 7.3 us
    all_to_all x5 -> x2, blocking collectives: 184 us -> 29.6 us  [exchange(): return lax.all_to_all(blocks, axes, 0, 0, tiled=False)]
    all_to_all x1 -> x3, starting transfers between devices: 4.85 us -> 45 us  [exchange(): return lax.all_to_all(blocks, axes, 0, 0, tiled=False)]
    ppermute x0 -> x6, starting transfers between devices: none -> 27.6 us  [flip(): lax.ppermute(block, QUAD, [(i, i ^ 2 * slab + column) for i in range(4)])]
    all_gather x0 -> x1, blocking collectives: none -> 14.3 us  [local(): near = lax.all_gather(far, NEAR, axis=0, tiled=True)]
    ppermute x0 -> x6, waiting for transfers between devices: none -> 11.5 us  [flip(): lax.ppermute(block, QUAD, [(i, i ^ 2 * slab + column) for i in range(4)])]
    all_to_all x1 -> x3, waiting for transfers between devices: 21.5 us -> 26.1 us  [exchange(): return lax.all_to_all(blocks, axes, 0, 0, tiled=False)]
    concatenate x2 -> x7, other arithmetic: 0.13 us -> 3.52 us  [the longest x3 2.63 us: local(): sent = jnp.concatenate([t.astype(BF16) for t in grads(s, c)])]
    dot_general x5 -> x20, matrix products: 4.69 us -> 7.3 us  [dot(): lax.dot_general(a, b, (((ca,), (cb,)), ((), ())), preferred_element_type=...]
  transfers between devices with their start and end apart: 1 -> 9, of which waited for: 1 -> 3; matrix products, arithmetic and copies ran while one was open for 1% -> 7% of each run, Pallas kernels for 0% -> 0%
where the time goes in v2:
time: 175 us; the launch traced here: 173 us
  starting transfers between devices  72.6 us (41%)
  blocking collectives  44 us (25%)
  waiting for transfers between devices  37.6 us (21%)
  matrix products  7.3 us (4%)
  other arithmetic  7.13 us (4%)
  local copies, waits for them, and re-layouts  3.22 us (2%)
    all_to_all x3, starting transfers between devices, exchange(): return lax.all_to_all(blocks, axes, 0, 0, tiled=False)  45 us
    all_to_all x2, blocking collectives, exchange(): return lax.all_to_all(blocks, axes, 0, 0, tiled=False)  29.6 us
    ppermute x6, starting transfers between devices, flip(): lax.ppermute(block, QUAD, [(i, i ^ 2 * slab + column) for i in range(4)])  27.6 us
    all_to_all x3, waiting for transfers between devices, exchange(): return lax.all_to_all(blocks, axes, 0, 0, tiled=False)  26.1 us
    all_gather x1, blocking collectives, local(): near = lax.all_gather(far, NEAR, axis=0, tiled=True)  14.3 us
    ppermute x6, waiting for transfers between devices, flip(): lax.ppermute(block, QUAD, [(i, i ^ 2 * slab + column) for i in range(4)])  11.5 us
    dot_general x20, matrix products, dot(): lax.dot_general(a, b, (((ca,), (cb,)), ((), ())), preferred_element_type=...  7.3 us
  transfers between devices with their start and end apart: 9, of which 3 were waited for; matrix products, arithmetic and copies ran while one was open for 7% of the time, Pallas kernels for 0%

profile of v2, /device:TPU:1, one launch (start us, length us, event | category | flops | bytes accessed | tf_op | source)
XLA Modules:
  0.0 172.8 jit_solution(17853806438957331828)
XLA Ops:
  0.6 0.8 maximum_bitcast_fusion
  1.4 0.7 broadcast_in_dim.4
  2.1 29.9 %all-to-all-start = ((bf16[16,2,8,384]{3,2,1,0:T(8,128)(2,1)}), bf16[16,2,8,384]{3,2,1,0:T(8,128)(2,1)S(1)}, u32[]{:S(2)}, u32[]{:S(2)}) async-start(bf16[16,2,8,384]{3,2,1,0:T(8,128)(2,1)} %bitcast.3), calls=%async_computation | async-start | bytes 393216 | tf_op jit(solution)/shard_map/all_to_all | solution.py:23
  32.0 1.7 constant_dynamic-update-slice_fusion.1
  33.7 0.7 constant_dynamic-update-slice_fusion
  34.4 3.1 %collective-permute-start.2 = (bf16[768,384]{1,0:T(8,128)(2,1)}, bf16[768,384]{1,0:T(8,128)(2,1)S(1)}, u32[]{:S(2)}, u32[]{:S(2)}) collective-permute-start(bf16[768,384]{1,0:T(8,128)(2,1)} %constant_dynamic-update-slice_fusion), channel_id=1, source_target_pairs={{0,96},{32,64},{64,32},{96,0},{1,97},{33,65},{65,33},{97,1},{2,98}... | collective-permute-start | bytes 1769480 | tf_op jit(solution)/shard_map/ppermute | solution.py:27
  37.5 2.2 %collective-permute-start.1 = (bf16[768,384]{1,0:T(8,128)(2,1)}, bf16[768,384]{1,0:T(8,128)(2,1)S(1)}, u32[]{:S(2)}, u32[]{:S(2)}) collective-permute-start(bf16[768,384]{1,0:T(8,128)(2,1)} %constant_dynamic-update-slice_fusion), channel_id=1, source_target_pairs={{0,32},{32,0},{64,96},{96,64},{1,33},{33,1},{65,97},{97,65},{2,34}... | collective-permute-start | bytes 1769480 | tf_op jit(solution)/shard_map/ppermute | solution.py:27
  39.7 2.6 %collective-permute-start = (bf16[768,384]{1,0:T(8,128)(2,1)}, bf16[768,384]{1,0:T(8,128)(2,1)S(1)}, u32[]{:S(2)}, u32[]{:S(2)}) collective-permute-start(bf16[768,384]{1,0:T(8,128)(2,1)} %constant_dynamic-update-slice_fusion), channel_id=1, source_target_pairs={{0,64},{32,96},{64,0},{96,32},{1,65},{33,97},{65,1},{97,33},{2,66}... | collective-permute-start | bytes 1769480 | tf_op jit(solution)/shard_map/ppermute | solution.py:27
  42.3 16.7 %all-to-all-done = bf16[16,2,8,384]{3,2,1,0:T(8,128)(2,1)S(1)} async-done(((bf16[16,2,8,384]{3,2,1,0:T(8,128)(2,1)}), bf16[16,2,8,384]{3,2,1,0:T(8,128)(2,1)S(1)}, u32[]{:S(2)}, u32[]{:S(2)}) %all-to-all-start) | async-done | bytes 196640 | tf_op jit(solution)/shard_map/all_to_all | solution.py:23
  59.1 14.3 %all_gather.3 = bf16[256,1536]{1,0:T(8,128)(2,1)S(1)} all-gather(bf16[64,1536]{1,0:T(8,128)(2,1)S(1)} %pad_maximum_fusion.5), channel_id=1, replica_groups=mesh['xh'=2,'y'=4,'core'=2,'xl'=2,'zh'=8,'zl'=4] {'zl'}, dimensions={0}, use_global_device_ids=true | all-gather | bytes 983040 | tf_op jit(solution)/shard_map/all_gather | solution.py:51
  75.1 0.3 fusion.2
  75.8 16.8 %all_to_all.25 = bf16[8,32,1536]{2,1,0:T(8,128)(2,1)S(1)} all-to-all(bf16[8,32,1536]{2,1,0:T(8,128)(2,1)S(1)} %bitcast.42), channel_id=1, replica_groups=mesh['xh'=2,'y'=4,'core'=2,'xl'=2,'zh'=8,'zl'=4] {'xh','y'}, dimensions={0} | all-to-all | bytes 1572864 | tf_op jit(solution)/shard_map/all_to_all | solution.py:23
  92.9 12.8 %all_to_all.26 = bf16[8,32,1536]{2,1,0:T(8,128)(2,1)S(1)} all-to-all(bf16[8,32,1536]{2,1,0:T(8,128)(2,1)S(1)} %broadcast_in_dim.5), channel_id=1, replica_groups=mesh['xh'=2,'y'=4,'core'=2,'xl'=2,'zh'=8,'zl'=4] {'xh','y'}, dimensions={0} | all-to-all | bytes 1572864 | tf_op jit(solution)/shard_map/all_to_all | solution.py:23
  106.3 0.3 fusion.5
  106.6 0.3 fusion.4
  106.9 0.8 pad_maximum_fusion.4
  107.7 4.4 %all-to-all-start.3 = ((bf16[4,64,768]{2,1,0:T(8,128)(2,1)}), bf16[4,64,768]{2,1,0:T(8,128)(2,1)S(1)}, u32[]{:S(2)}, u32[]{:S(2)}) async-start(bf16[4,64,768]{2,1,0:T(8,128)(2,1)} %bitcast.13), calls=%async_computation.3 | async-start | bytes 786432 | tf_op jit(solution)/shard_map/all_to_all | solution.py:23
  112.6 0.9 pad_maximum_fusion.1
  113.5 14.3 %collective-permute-start.3 = (bf16[768,384]{1,0:T(8,128)(2,1)}, bf16[768,384]{1,0:T(8,128)(2,1)S(1)}, u32[]{:S(2)}, u32[]{:S(2)}) collective-permute-start(bf16[768,384]{1,0:T(8,128)(2,1)} %pad_maximum_fusion.1), channel_id=1, source_target_pairs={{0,64},{32,96},{64,0},{96,32},{1,65},{33,97},{65,1},{97,33},{2,66}... | collective-permute-start | bytes 1769480 | tf_op jit(solution)/shard_map/ppermute | solution.py:27
  128.4 0.9 pad_maximum_fusion.2
  129.3 2.2 %collective-permute-start.4 = (bf16[768,384]{1,0:T(8,128)(2,1)}, bf16[768,384]{1,0:T(8,128)(2,1)S(1)}, u32[]{:S(2)}, u32[]{:S(2)}) collective-permute-start(bf16[768,384]{1,0:T(8,128)(2,1)} %pad_maximum_fusion.2), channel_id=1, source_target_pairs={{0,32},{32,0},{64,96},{96,64},{1,33},{33,1},{65,97},{97,65},{2,34}... | collective-permute-start | bytes 1769480 | tf_op jit(solution)/shard_map/ppermute | solution.py:27
  131.5 0.3 convolution_convert_fusion.1
  132.1 0.9 pad_maximum_fusion.3
  133.0 3.2 %collective-permute-start.5 = (bf16[768,384]{1,0:T(8,128)(2,1)}, bf16[768,384]{1,0:T(8,128)(2,1)}, u32[]{:S(2)}, u32[]{:S(2)}) collective-permute-start(bf16[768,384]{1,0:T(8,128)(2,1)} %pad_maximum_fusion.3), channel_id=1, source_target_pairs={{0,96},{32,64},{64,32},{96,0},{1,97},{33,65},{65,33},{97,1},{2,98}... | collective-permute-start | bytes 1769480 | tf_op jit(solution)/shard_map/ppermute | solution.py:27
  136.3 0.7 pad_maximum_fusion.7
  137.0 10.7 %all-to-all-start.4 = ((bf16[16,8,384]{2,1,0:T(8,128)(2,1)}), bf16[16,8,384]{2,1,0:T(8,128)(2,1)S(1)}, u32[]{:S(2)}, u32[]{:S(2)}) async-start(bf16[16,8,384]{2,1,0:T(8,128)(2,1)} %bitcast.16), calls=%async_computation.4 | async-start | bytes 196608 | tf_op jit(solution)/shard_map/all_to_all | solution.py:23
  147.9 11.5 %collective-permute-done.5 = bf16[768,384]{1,0:T(8,128)(2,1)} collective-permute-done((bf16[768,384]{1,0:T(8,128)(2,1)}, bf16[768,384]{1,0:T(8,128)(2,1)}, u32[]{:S(2)}, u32[]{:S(2)}) %collective-permute-start.5) | collective-permute-done | bytes 589856 | tf_op jit(solution)/shard_map/ppermute | solution.py:27
  159.4 1.1 convert_element_type.75
  160.5 1.1 slice_add_fusion
  161.6 1.1 slice_add_fusion.3
  162.8 9.4 %all-to-all-done.4 = bf16[16,8,384]{2,1,0:T(8,128)(2,1)S(1)} async-done(((bf16[16,8,384]{2,1,0:T(8,128)(2,1)}), bf16[16,8,384]{2,1,0:T(8,128)(2,1)S(1)}, u32[]{:S(2)}, u32[]{:S(2)}) %all-to-all-start.4) | async-done | bytes 98336 | tf_op jit(solution)/shard_map/all_to_all | solution.py:23
  172.2 0.6 bitcast_reduce_fusion
  (36 shorter events, 4.5 us)
Async XLA Ops:
  0.6 33.1 %copy-start.1 = (bf16[384,384]{1,0:T(8,128)(2,1)S(1)}, bf16[384,384]{1,0:T(8,128)(2,1)}, u32[]{:S(2)}) copy-start(bf16[384,384]{1,0:T(8,128)(2,1)} %param.7) | copy-start | bytes 884740
  2.1 56.9 %all-to-all-start = ((bf16[16,2,8,384]{3,2,1,0:T(8,128)(2,1)}), bf16[16,2,8,384]{3,2,1,0:T(8,128)(2,1)S(1)}, u32[]{:S(2)}, u32[]{:S(2)}) async-start(bf16[16,2,8,384]{3,2,1,0:T(8,128)(2,1)} %bitcast.3), calls=%async_computation | async-start | bytes 393216 | tf_op jit(solution)/shard_map/all_to_all | solution.py:23
  34.4 39.5 %collective-permute-start.2 = (bf16[768,384]{1,0:T(8,128)(2,1)}, bf16[768,384]{1,0:T(8,128)(2,1)S(1)}, u32[]{:S(2)}, u32[]{:S(2)}) collective-permute-start(bf16[768,384]{1,0:T(8,128)(2,1)} %constant_dynamic-update-slice_fusion), channel_id=1, source_target_pairs={{0,96},{32,64},{64,32},{96,0},{1,97},{33,65},{65,33},{97,1},{2,98}... | collective-permute-start | bytes 1769480 | tf_op jit(solution)/shard_map/ppermute | solution.py:27
  37.5 37.0 %collective-permute-start.1 = (bf16[768,384]{1,0:T(8,128)(2,1)}, bf16[768,384]{1,0:T(8,128)(2,1)S(1)}, u32[]{:S(2)}, u32[]{:S(2)}) collective-permute-start(bf16[768,384]{1,0:T(8,128)(2,1)} %constant_dynamic-update-slice_fusion), channel_id=1, source_target_pairs={{0,32},{32,0},{64,96},{96,64},{1,33},{33,1},{65,97},{97,65},{2,34}... | collective-permute-start | bytes 1769480 | tf_op jit(solution)/shard_map/ppermute | solution.py:27
  39.7 35.4 %collective-permute-start = (bf16[768,384]{1,0:T(8,128)(2,1)}, bf16[768,384]{1,0:T(8,128)(2,1)S(1)}, u32[]{:S(2)}, u32[]{:S(2)}) collective-permute-start(bf16[768,384]{1,0:T(8,128)(2,1)} %constant_dynamic-update-slice_fusion), channel_id=1, source_target_pairs={{0,64},{32,96},{64,0},{96,32},{1,65},{33,97},{65,1},{97,33},{2,66}... | collective-permute-start | bytes 1769480 | tf_op jit(solution)/shard_map/ppermute | solution.py:27
  59.0 14.7 %copy-start = (bf16[384,384]{1,0:T(8,128)(2,1)S(1)}, bf16[384,384]{1,0:T(8,128)(2,1)}, u32[]{:S(2)}) copy-start(bf16[384,384]{1,0:T(8,128)(2,1)} %param.6) | copy-start | bytes 884740
  107.7 28.6 %all-to-all-start.3 = ((bf16[4,64,768]{2,1,0:T(8,128)(2,1)}), bf16[4,64,768]{2,1,0:T(8,128)(2,1)S(1)}, u32[]{:S(2)}, u32[]{:S(2)}) async-start(bf16[4,64,768]{2,1,0:T(8,128)(2,1)} %bitcast.13), calls=%async_computation.3 | async-start | bytes 786432 | tf_op jit(solution)/shard_map/all_to_all | solution.py:23
  113.5 34.2 %collective-permute-start.3 = (bf16[768,384]{1,0:T(8,128)(2,1)}, bf16[768,384]{1,0:T(8,128)(2,1)S(1)}, u32[]{:S(2)}, u32[]{:S(2)}) collective-permute-start(bf16[768,384]{1,0:T(8,128)(2,1)} %pad_maximum_fusion.1), channel_id=1, source_target_pairs={{0,64},{32,96},{64,0},{96,32},{1,65},{33,97},{65,1},{97,33},{2,66}... | collective-permute-start | bytes 1769480 | tf_op jit(solution)/shard_map/ppermute | solution.py:27
  129.3 18.5 %collective-permute-start.4 = (bf16[768,384]{1,0:T(8,128)(2,1)}, bf16[768,384]{1,0:T(8,128)(2,1)S(1)}, u32[]{:S(2)}, u32[]{:S(2)}) collective-permute-start(bf16[768,384]{1,0:T(8,128)(2,1)} %pad_maximum_fusion.2), channel_id=1, source_target_pairs={{0,32},{32,0},{64,96},{96,64},{1,33},{33,1},{65,97},{97,65},{2,34}... | collective-permute-start | bytes 1769480 | tf_op jit(solution)/shard_map/ppermute | solution.py:27
  133.0 26.4 %collective-permute-start.5 = (bf16[768,384]{1,0:T(8,128)(2,1)}, bf16[768,384]{1,0:T(8,128)(2,1)}, u32[]{:S(2)}, u32[]{:S(2)}) collective-permute-start(bf16[768,384]{1,0:T(8,128)(2,1)} %pad_maximum_fusion.3), channel_id=1, source_target_pairs={{0,96},{32,64},{64,32},{96,0},{1,97},{33,65},{65,33},{97,1},{2,98}... | collective-permute-start | bytes 1769480 | tf_op jit(solution)/shard_map/ppermute | solution.py:27
  137.0 35.2 %all-to-all-start.4 = ((bf16[16,8,384]{2,1,0:T(8,128)(2,1)}), bf16[16,8,384]{2,1,0:T(8,128)(2,1)S(1)}, u32[]{:S(2)}, u32[]{:S(2)}) async-start(bf16[16,8,384]{2,1,0:T(8,128)(2,1)} %bitcast.16), calls=%async_computation.4 | async-start | bytes 196608 | tf_op jit(solution)/shard_map/all_to_all | solution.py:23

commit v3 on v2

--- a/solution.py
+++ b/solution.py
@@ -7,7 +7,7 @@
 
 QUAD = ("core", "xl")
 PLANE = ("xh", "y")
-FAR = ("core", "zh")
+SPAN = ("core", "zh", "zl")
 NEAR = ("zl",)
 F32 = jnp.float32
 BF16 = jnp.bfloat16
@@ -21,6 +21,13 @@
 
 def exchange(blocks, axes):
     return lax.all_to_all(blocks, axes, 0, 0, tiled=False)
+
+
+def exchange_far(blocks):
+    groups = [
+        [c * 32 + (z + 4) % 8 * 4 + low for c in range(2) for z in range(8)] for low in range(4)
+    ]
+    return lax.all_to_all(blocks, SPAN, 0, 0, axis_index_groups=groups, tiled=False)
 
 
 def flip(block, slab, column):
@@ -43,7 +50,7 @@
 
     pair = jnp.stack([inputs, out_grad]).reshape(2, 2, half, width).transpose(1, 0, 2, 3)
     pair = jnp.broadcast_to(pair[:, None], (2, 8, 2, half, width))
-    far = exchange(pair.reshape(16, 2, half, width), FAR).reshape(2, 8, 2, half, width)
+    far = exchange_far(pair.reshape(16, 2, half, width)).reshape(2, 8, 2, half, width)
     far = far.transpose(2, 0, 1, 3, 4).reshape(2, 2, 8 * half, width)
     own_in, own_grad = [jnp.where(core == 0, f[0], f[1]) for f in far]
     other_in, other_grad = [jnp.where(core == 0, f[1], f[0]) for f in far]
@@ -69,22 +76,26 @@
 
     terms = [dot(d_pre[0], first[s][0], 1, 1) + dot(d_pre[1], first[s][1], 1, 1) for s in range(2)]
     terms = jnp.concatenate([t.astype(BF16) for t in terms], axis=1)
+
+    def grads(s, c):
+        return [dot(x[s], d_pre[c], 0, 0), dot(act[c], g[s], 0, 0)]
+
+    sent = jnp.concatenate([t.astype(BF16) for c in range(2) for t in grads(1, c)])
+    terms, sent = lax.optimization_barrier((terms, sent))
+    came = flip(sent, 1, 0).reshape(2, 2, width, width).astype(F32)
+    kept = [[t + came[c, i] for i, t in enumerate(grads(0, c))] for c in range(2)]
+    mixed = jnp.concatenate([t.astype(BF16) for t in kept[1]])
+
     terms = exchange(terms.reshape(4, tokens // 4, 2 * width), NEAR)
     terms = jnp.sum(terms.astype(F32), axis=0).astype(BF16)
     own, other = terms[:, :width], terms[:, width:]
     terms = jnp.stack([jnp.where(core == 0, own, other), jnp.where(core == 0, other, own)])
-    terms = exchange(terms.reshape(16, half, width), FAR).reshape(2, 8, half, width)
+    terms = exchange_far(terms.reshape(16, half, width)).reshape(2, 8, half, width)
     d_input = jnp.sum(terms.astype(F32), axis=1).astype(BF16).reshape(rows, width)
 
-    def grads(s, c):
-        return (dot(x[s], d_pre[c], 0, 0), dot(act[c], g[s], 0, 0))
-
-    grad_first, grad_second = grads(0, 0)
-    for s, c in ((1, 0), (0, 1), (1, 1)):
-        sent = jnp.concatenate([t.astype(BF16) for t in grads(s, c)])
-        came = flip(sent, s, c).astype(F32)
-        grad_first = grad_first + came[:width]
-        grad_second = grad_second + came[width:]
+    came = flip(mixed, 0, 1)
+    grad_first = kept[0][0] + came[:width].astype(F32)
+    grad_second = kept[0][1] + came[width:].astype(F32)
     return (d_input, grad_first, grad_second)
 
 

time: 175 us -> 164 us (0.937)
  waiting for transfers between devices: 37.6 us -> 13.7 us
  starting transfers between devices: 72.6 us -> 83.2 us
  matrix products: 7.3 us -> 9.52 us
  local copies, waits for them, and re-layouts: 3.22 us -> 5.24 us
    all_to_all x0 -> x2, starting transfers between devices: none -> 61 us  [exchange_far(): lax.all_to_all(blocks, SPAN, 0, 0, axis_index_groups=groups, tiled=False)]
    all_to_all x3 -> x1, starting transfers between devices: 45 us -> 5.12 us  [exchange(): return lax.all_to_all(blocks, axes, 0, 0, tiled=False)]
    all_to_all x3 -> x1, waiting for transfers between devices: 26.1 us -> 0.01 us  [exchange(): return lax.all_to_all(blocks, axes, 0, 0, tiled=False)]
    all_to_all x0 -> x2, waiting for transfers between devices: none -> 11.2 us  [exchange_far(): lax.all_to_all(blocks, SPAN, 0, 0, axis_index_groups=groups, tiled=False)]
    ppermute x6 -> x5, starting transfers between devices: 27.6 us -> 17 us  [flip(): lax.ppermute(block, QUAD, [(i, i ^ 2 * slab + column) for i in range(4)])]
    ppermute x6 -> x5, waiting for transfers between devices: 11.5 us -> 2.46 us  [flip(): lax.ppermute(block, QUAD, [(i, i ^ 2 * slab + column) for i in range(4)])]
    dot_general x20, matrix products: 7.3 us -> 9.52 us  [dot(): lax.dot_general(a, b, (((ca,), (cb,)), ((), ())), preferred_element_type=...]
  transfers between devices with their start and end apart: 9 -> 8, of which waited for: 3 -> 3; matrix products, arithmetic and copies ran while one was open for 7% -> 8% of each run, Pallas kernels for 0% -> 0%
where the time goes in v3:
time: 164 us; the launch traced here: 163 us
  starting transfers between devices  83.2 us (51%)
  blocking collectives  45.2 us (28%)
  waiting for transfers between devices  13.7 us (8%)
  matrix products  9.52 us (6%)
  other arithmetic  5.75 us (4%)
  local copies, waits for them, and re-layouts  5.24 us (3%)
    all_to_all x2, starting transfers between devices, exchange_far(): lax.all_to_all(blocks, SPAN, 0, 0, axis_index_groups=groups, tiled=False)  61 us
    all_to_all x2, blocking collectives, exchange(): return lax.all_to_all(blocks, axes, 0, 0, tiled=False)  29.8 us
    ppermute x5, starting transfers between devices, flip(): lax.ppermute(block, QUAD, [(i, i ^ 2 * slab + column) for i in range(4)])  17 us
    all_gather x1, blocking collectives, local(): near = lax.all_gather(far, NEAR, axis=0, tiled=True)  15.4 us
    all_to_all x2, waiting for transfers between devices, exchange_far(): lax.all_to_all(blocks, SPAN, 0, 0, axis_index_groups=groups, tiled=False)  11.2 us
    dot_general x20, matrix products, dot(): lax.dot_general(a, b, (((ca,), (cb,)), ((), ())), preferred_element_type=...  9.52 us
    all_to_all x1, starting transfers between devices, exchange(): return lax.all_to_all(blocks, axes, 0, 0, tiled=False)  5.12 us
  transfers between devices with their start and end apart: 8, of which 3 were waited for; matrix products, arithmetic and copies ran while one was open for 8% of the time, Pallas kernels for 0%

profile of v3, /device:TPU:1, one launch (start us, length us, event | category | flops | bytes accessed | tf_op | source)
XLA Modules:
  0.0 163.5 jit_solution(947872852830554371)
XLA Ops:
  0.6 0.7 maximum_bitcast_fusion
  1.4 0.7 broadcast_in_dim.4
  2.1 35.5 %all-to-all-start = ((bf16[16,2,8,384]{3,2,1,0:T(8,128)(2,1)}), bf16[16,2,8,384]{3,2,1,0:T(8,128)(2,1)S(1)}, u32[]{:S(2)}, u32[]{:S(2)}) async-start(bf16[16,2,8,384]{3,2,1,0:T(8,128)(2,1)} %bitcast.3), calls=%async_computation | async-start | bytes 393216 | tf_op jit(solution)/shard_map/all_to_all | solution.py:30
  37.6 1.8 %constant_dynamic-update-slice_fusion.1 = bf16[768,384]{1,0:T(8,128)(2,1)} fusion(bf16[384,384]{1,0:T(8,128)(2,1)} %param.6), kind=kLoop, calls=%fused_computation.101 | loop fusion | bytes 589824
  39.3 1.7 %constant_dynamic-update-slice_fusion = bf16[768,384]{1,0:T(8,128)(2,1)} fusion(bf16[768,384]{1,0:T(8,128)(2,1)} %constant_dynamic-update-slice_fusion.1, bf16[384,384]{1,0:T(8,128)(2,1)} %param.7), kind=kLoop, calls=%fused_computation.100 | loop fusion | bytes 589824 | tf_op jit(solution)/shard_map/concatenate | solution.py:46
  41.1 3.4 %collective-permute-start.2 = (bf16[768,384]{1,0:T(8,128)(2,1)}, bf16[768,384]{1,0:T(8,128)(2,1)S(1)}, u32[]{:S(2)}, u32[]{:S(2)}) collective-permute-start(bf16[768,384]{1,0:T(8,128)(2,1)} %constant_dynamic-update-slice_fusion), channel_id=1, source_target_pairs={{0,96},{32,64},{64,32},{96,0},{1,97},{33,65},{65,33},{97,1},{2,98}... | collective-permute-start | bytes 1769480 | tf_op jit(solution)/shard_map/ppermute | solution.py:34
  44.5 2.2 %collective-permute-start.1 = (bf16[768,384]{1,0:T(8,128)(2,1)}, bf16[768,384]{1,0:T(8,128)(2,1)S(1)}, u32[]{:S(2)}, u32[]{:S(2)}) collective-permute-start(bf16[768,384]{1,0:T(8,128)(2,1)} %constant_dynamic-update-slice_fusion), channel_id=1, source_target_pairs={{0,32},{32,0},{64,96},{96,64},{1,33},{33,1},{65,97},{97,65},{2,34}... | collective-permute-start | bytes 1769480 | tf_op jit(solution)/shard_map/ppermute | solution.py:34
  46.6 2.4 %collective-permute-start = (bf16[768,384]{1,0:T(8,128)(2,1)}, bf16[768,384]{1,0:T(8,128)(2,1)S(1)}, u32[]{:S(2)}, u32[]{:S(2)}) collective-permute-start(bf16[768,384]{1,0:T(8,128)(2,1)} %constant_dynamic-update-slice_fusion), channel_id=1, source_target_pairs={{0,64},{32,96},{64,0},{96,32},{1,65},{33,97},{65,1},{97,33},{2,66}... | collective-permute-start | bytes 1769480 | tf_op jit(solution)/shard_map/ppermute | solution.py:34
  49.0 6.6 %all-to-all-done = bf16[16,2,8,384]{3,2,1,0:T(8,128)(2,1)S(1)} async-done(((bf16[16,2,8,384]{3,2,1,0:T(8,128)(2,1)}), bf16[16,2,8,384]{3,2,1,0:T(8,128)(2,1)S(1)}, u32[]{:S(2)}, u32[]{:S(2)}) %all-to-all-start) | async-done | bytes 196640 | tf_op jit(solution)/shard_map/all_to_all | solution.py:30
  55.6 15.4 %all_gather.3 = bf16[256,1536]{1,0:T(8,128)(2,1)S(1)} all-gather(bf16[64,1536]{1,0:T(8,128)(2,1)S(1)} %pad_maximum_fusion.4), channel_id=1, replica_groups=mesh['xh'=2,'y'=4,'core'=2,'xl'=2,'zh'=8,'zl'=4] {'zl'}, dimensions={0}, use_global_device_ids=true | all-gather | bytes 983040 | tf_op jit(solution)/shard_map/all_gather | solution.py:58
  73.4 16.9 %all_to_all.25 = bf16[8,32,1536]{2,1,0:T(8,128)(2,1)S(1)} all-to-all(bf16[8,32,1536]{2,1,0:T(8,128)(2,1)S(1)} %bitcast.68), channel_id=1, replica_groups=mesh['xh'=2,'y'=4,'core'=2,'xl'=2,'zh'=8,'zl'=4] {'xh','y'}, dimensions={0} | all-to-all | bytes 1572864 | tf_op jit(solution)/shard_map/all_to_all | solution.py:23
  90.6 12.8 %all_to_all.26 = bf16[8,32,1536]{2,1,0:T(8,128)(2,1)S(1)} all-to-all(bf16[8,32,1536]{2,1,0:T(8,128)(2,1)S(1)} %broadcast_in_dim.5), channel_id=1, replica_groups=mesh['xh'=2,'y'=4,'core'=2,'xl'=2,'zh'=8,'zl'=4] {'xh','y'}, dimensions={0} | all-to-all | bytes 1572864 | tf_op jit(solution)/shard_map/all_to_all | solution.py:23
  103.8 0.3 convolution_convert_fusion.1
  104.1 0.3 convolution_convert_fusion
  104.4 0.3 convolution_convert_fusion.2
  105.9 0.8 pad_maximum_fusion.3
  106.8 5.1 %all-to-all-start.3 = ((bf16[4,64,768]{2,1,0:T(8,128)(2,1)}), bf16[4,64,768]{2,1,0:T(8,128)(2,1)S(1)}, u32[]{:S(2)}, u32[]{:S(2)}) async-start(bf16[4,64,768]{2,1,0:T(8,128)(2,1)} %bitcast.13), calls=%async_computation.3 | async-start | bytes 786432 | tf_op jit(solution)/shard_map/all_to_all | solution.py:23
  111.9 7.0 %collective-permute-start.3 = (bf16[1536,384]{1,0:T(8,128)(2,1)S(1)}, bf16[1536,384]{1,0:T(8,128)(2,1)S(1)}, u32[]{:S(2)}, u32[]{:S(2)}) collective-permute-start(bf16[1536,384]{1,0:T(8,128)(2,1)S(1)} %pad_maximum_fusion), channel_id=1, source_target_pairs={{0,64},{32,96},{64,0},{96,32},{1,65},{33,97},{65,1},{97,33},{2,66}... | collective-permute-start | bytes 3538952 | tf_op jit(solution)/shard_map/ppermute | solution.py:34
  118.9 2.5 %collective-permute-done.3 = bf16[1536,384]{1,0:T(8,128)(2,1)S(1)} collective-permute-done((bf16[1536,384]{1,0:T(8,128)(2,1)S(1)}, bf16[1536,384]{1,0:T(8,128)(2,1)S(1)}, u32[]{:S(2)}, u32[]{:S(2)}) %collective-permute-start.3) | collective-permute-done | bytes 1179680 | tf_op jit(solution)/shard_map/ppermute | solution.py:34
  121.5 1.0 copy-done.1
  122.5 0.3 fusion.9
  122.8 0.3 fusion.11
  123.1 0.9 pad_maximum_fusion.2
  124.0 2.2 %collective-permute-start.4 = (bf16[768,384]{1,0:T(8,128)(2,1)}, bf16[768,384]{1,0:T(8,128)(2,1)}, u32[]{:S(2)}, u32[]{:S(2)}) collective-permute-start(bf16[768,384]{1,0:T(8,128)(2,1)} %pad_maximum_fusion.2), channel_id=1, source_target_pairs={{0,32},{32,0},{64,96},{96,64},{1,33},{33,1},{65,97},{97,65},{2,34}... | collective-permute-start | bytes 1769480 | tf_op jit(solution)/shard_map/ppermute | solution.py:34
  126.2 0.7 reduce_sum.34
  126.9 0.8 select_bitcast_fusion.1
  127.7 0.7 pad_maximum_fusion.6
  128.4 25.5 %all-to-all-start.4 = ((bf16[16,8,384]{2,1,0:T(8,128)(2,1)}), bf16[16,8,384]{2,1,0:T(8,128)(2,1)S(1)}, u32[]{:S(2)}, u32[]{:S(2)}) async-start(bf16[16,8,384]{2,1,0:T(8,128)(2,1)} %bitcast.16), calls=%async_computation.4 | async-start | bytes 196608 | tf_op jit(solution)/shard_map/all_to_all | solution.py:30
  153.9 2.2 %fusion.7 = f32[384,384]{1,0:T(8,128)} fusion(f32[2,2,384,384]{3,2,1,0:T(8,128)S(1)} %convert.3, bf16[768,384]{1,0:T(8,128)(2,1)} %collective-permute-done.4, bf16[256,1536]{1,0:T(8,128)(2,1)} %bitcast.64, bf16[256,1536]{1,0:T(8,128)(2,1)S(1)} %all_gather.3), kind=kOutput, calls=%fused_computation.21 | convolution fusion | flops 75939840 | bytes 1867776 | tf_op jit(solution)/shard_map/dot_general | solution.py:38
  156.1 2.2 %fusion.13 = f32[384,384]{1,0:T(8,128)} fusion(f32[2,2,384,384]{3,2,1,0:T(8,128)S(1)} %convert.3, bf16[768,384]{1,0:T(8,128)(2,1)} %collective-permute-done.4, bf16[256,1536]{1,0:T(8,128)(2,1)} %bitcast.65, bf16[256,1536]{1,0:T(8,128)(2,1)S(1)} %all_gather.3), kind=kOutput, calls=%fused_computation.30 | convolution fusion | flops 75939840 | bytes 1867776 | tf_op jit(solution)/shard_map/dot_general | solution.py:38
  158.2 4.6 %all-to-all-done.4 = bf16[16,8,384]{2,1,0:T(8,128)(2,1)S(1)} async-done(((bf16[16,8,384]{2,1,0:T(8,128)(2,1)}), bf16[16,8,384]{2,1,0:T(8,128)(2,1)S(1)}, u32[]{:S(2)}, u32[]{:S(2)}) %all-to-all-start.4) | async-done | bytes 98336 | tf_op jit(solution)/shard_map/all_to_all | solution.py:30
  162.9 0.6 bitcast_reduce_fusion
  (35 shorter events, 4.3 us)
Async XLA Ops:
  2.1 53.5 %all-to-all-start = ((bf16[16,2,8,384]{3,2,1,0:T(8,128)(2,1)}), bf16[16,2,8,384]{3,2,1,0:T(8,128)(2,1)S(1)}, u32[]{:S(2)}, u32[]{:S(2)}) async-start(bf16[16,2,8,384]{3,2,1,0:T(8,128)(2,1)} %bitcast.3), calls=%async_computation | async-start | bytes 393216 | tf_op jit(solution)/shard_map/all_to_all | solution.py:30
  37.6 33.5 %copy-start.3 = (bf16[384,384]{1,0:T(8,128)(2,1)S(1)}, bf16[384,384]{1,0:T(8,128)(2,1)}, u32[]{:S(2)}) copy-start(bf16[384,384]{1,0:T(8,128)(2,1)} %param.7) | copy-start | bytes 884740
  39.3 32.0 %copy-start.2 = (bf16[384,384]{1,0:T(8,128)(2,1)S(1)}, bf16[384,384]{1,0:T(8,128)(2,1)}, u32[]{:S(2)}) copy-start(bf16[384,384]{1,0:T(8,128)(2,1)} %param.6) | copy-start | bytes 884740
  41.1 30.5 %collective-permute-start.2 = (bf16[768,384]{1,0:T(8,128)(2,1)}, bf16[768,384]{1,0:T(8,128)(2,1)S(1)}, u32[]{:S(2)}, u32[]{:S(2)}) collective-permute-start(bf16[768,384]{1,0:T(8,128)(2,1)} %constant_dynamic-update-slice_fusion), channel_id=1, source_target_pairs={{0,96},{32,64},{64,32},{96,0},{1,97},{33,65},{65,33},{97,1},{2,98}... | collective-permute-start | bytes 1769480 | tf_op jit(solution)/shard_map/ppermute | solution.py:34
  44.5 27.7 %collective-permute-start.1 = (bf16[768,384]{1,0:T(8,128)(2,1)}, bf16[768,384]{1,0:T(8,128)(2,1)S(1)}, u32[]{:S(2)}, u32[]{:S(2)}) collective-permute-start(bf16[768,384]{1,0:T(8,128)(2,1)} %constant_dynamic-update-slice_fusion), channel_id=1, source_target_pairs={{0,32},{32,0},{64,96},{96,64},{1,33},{33,1},{65,97},{97,65},{2,34}... | collective-permute-start | bytes 1769480 | tf_op jit(solution)/shard_map/ppermute | solution.py:34
  46.6 26.2 %collective-permute-start = (bf16[768,384]{1,0:T(8,128)(2,1)}, bf16[768,384]{1,0:T(8,128)(2,1)S(1)}, u32[]{:S(2)}, u32[]{:S(2)}) collective-permute-start(bf16[768,384]{1,0:T(8,128)(2,1)} %constant_dynamic-update-slice_fusion), channel_id=1, source_target_pairs={{0,64},{32,96},{64,0},{96,32},{1,65},{33,97},{65,1},{97,33},{2,66}... | collective-permute-start | bytes 1769480 | tf_op jit(solution)/shard_map/ppermute | solution.py:34
  103.5 2.1 %copy-start = (bf16[8,32,1536]{2,1,0:T(8,128)(2,1)}, bf16[8,32,1536]{2,1,0:T(8,128)(2,1)S(1)}, u32[]{:S(2)}) copy-start(bf16[8,32,1536]{2,1,0:T(8,128)(2,1)S(1)} %all_to_all.26) | copy-start | bytes 2359300
  106.8 19.4 %all-to-all-start.3 = ((bf16[4,64,768]{2,1,0:T(8,128)(2,1)}), bf16[4,64,768]{2,1,0:T(8,128)(2,1)S(1)}, u32[]{:S(2)}, u32[]{:S(2)}) async-start(bf16[4,64,768]{2,1,0:T(8,128)(2,1)} %bitcast.13), calls=%async_computation.3 | async-start | bytes 786432 | tf_op jit(solution)/shard_map/all_to_all | solution.py:23
  111.9 9.4 %collective-permute-start.3 = (bf16[1536,384]{1,0:T(8,128)(2,1)S(1)}, bf16[1536,384]{1,0:T(8,128)(2,1)S(1)}, u32[]{:S(2)}, u32[]{:S(2)}) collective-permute-start(bf16[1536,384]{1,0:T(8,128)(2,1)S(1)} %pad_maximum_fusion), channel_id=1, source_target_pairs={{0,64},{32,96},{64,0},{96,32},{1,65},{33,97},{65,1},{97,33},{2,66}... | collective-permute-start | bytes 3538952 | tf_op jit(solution)/shard_map/ppermute | solution.py:34
  121.3 1.1 copy-start.1
  124.0 29.9 %collective-permute-start.4 = (bf16[768,384]{1,0:T(8,128)(2,1)}, bf16[768,384]{1,0:T(8,128)(2,1)}, u32[]{:S(2)}, u32[]{:S(2)}) collective-permute-start(bf16[768,384]{1,0:T(8,128)(2,1)} %pad_maximum_fusion.2), channel_id=1, source_target_pairs={{0,32},{32,0},{64,96},{96,64},{1,33},{33,1},{65,97},{97,65},{2,34}... | collective-permute-start | bytes 1769480 | tf_op jit(solution)/shard_map/ppermute | solution.py:34
  128.4 34.5 %all-to-all-start.4 = ((bf16[16,8,384]{2,1,0:T(8,128)(2,1)}), bf16[16,8,384]{2,1,0:T(8,128)(2,1)S(1)}, u32[]{:S(2)}, u32[]{:S(2)}) async-start(bf16[16,8,384]{2,1,0:T(8,128)(2,1)} %bitcast.16), calls=%async_computation.4 | async-start | bytes 196608 | tf_op jit(solution)/shard_map/all_to_all | solution.py:30

commit v4 on v3

v4 whole, which is shorter than its diff:
```python
import functools
import math

import jax
import jax.numpy as jnp
from jax import lax
from jax.experimental import pallas as pl
from jax.experimental.pallas import tpu as pltpu
from jax.sharding import Mesh, PartitionSpec as P

QUAD = ("core", "xl")
PLANE = ("xh", "y")
LIMIT = 16
COST = pl.CostEstimate(flops=30 * 10**9, bytes_accessed=2**22, transcendentals=0)
BOUND = pl.CostEstimate(flops=10**9, bytes_accessed=2**10, transcendentals=0)
SPAN = ("core", "zh", "zl")
NEAR = ("zl",)
F32 = jnp.float32
BF16 = jnp.bfloat16


def gelu_pair(pre):
    cdf = 0.5 * (1.0 + jax.scipy.special.erf(pre / math.sqrt(2.0)))
    dens = jnp.exp(-0.5 * pre * pre) / math.sqrt(2.0 * math.pi)
    return (pre * cdf, cdf + pre * dens)


def exchange(blocks, axes):
    return lax.all_to_all(blocks, axes, 0, 0, tiled=False)


def exchange_far(blocks):
    groups = [
        [c * 32 + z * 4 + low for z in (4, 0, 1, 7, 2, 6, 3, 5) for c in range(2)] for low in range(4)
    ]
    return lax.all_to_all(blocks, SPAN, 0, 0, axis_index_groups=groups, tiled=False)


def flip(block, slab, column):
    return lax.ppermute(block, QUAD, [(i, i ^ (2 * slab + column)) for i in range(4)])


def dot(a, b, ca, cb):
    return lax.dot_general(a, b, (((ca,), (cb,)), ((), ())), preferred_element_type=F32)


def call(kernel, outs, *operands, scalars=0, far=0, cost=None):
    specs = [pl.BlockSpec(memory_space=pltpu.SMEM)] * scalars
    specs += [pl.BlockSpec(memory_space=pltpu.VMEM)] * (len(operands) - scalars)
    out_specs = [pl.BlockSpec(memory_space=pltpu.HBM)] * far
    out_specs += [pl.BlockSpec(memory_space=pltpu.VMEM)] * (len(outs) - far)
    scratch = [pltpu.VMEM(shape, kind) for shape, kind in outs[:far]]
    scratch += [pltpu.SemaphoreType.DMA] * far
    return pl.pallas_call(
        kernel,
        out_shape=[jax.ShapeDtypeStruct(shape, kind) for shape, kind in outs],
        in_specs=specs,
        out_specs=out_specs,
        scratch_shapes=scratch,
        cost_estimate=cost,
        compiler_params=pltpu.CompilerParams(vmem_limit_bytes=LIMIT * 2**20),
    )(*operands)


def act_kernel(parts, out, held, done):
    half = parts.shape[2] // 2
    sums = parts[0].astype(F32)
    for i in range(1, 8):
        sums += parts[i].astype(F32)
    value, slope = gelu_pair(sums[:, :half])
    value = value.astype(BF16)
    slope = (sums[:, half:] * slope).astype(BF16)
    for i in range(8):
        held[i, :, :half] = value
        held[i, :, half:] = slope
    copy = pltpu.make_async_copy(held, out, done)
    copy.start()
    copy.wait()


def sum_kernel(terms, out, held, done):
    sums = terms[0].astype(F32)
    for i in range(1, 4):
        sums += terms[i].astype(F32)
    width = sums.shape[1] // 2
    for a in range(2):
        held[:, a] = sums[:, a * width : (a + 1) * width].reshape(8, 8, width).astype(BF16)
    copy = pltpu.make_async_copy(held, out, done)
    copy.start()
    copy.wait()


def forward_kernel(*refs):
    pieces, (w00, w01, w10, w11, near, parts) = refs[:-6], refs[-6:]
    at = 0
    for piece in pieces:
        near[at : at + piece.shape[0]] = piece[...]
        at += piece.shape[0]
    width = w00.shape[1]
    for c, (own, other) in enumerate(((w00, w10), (w01, w11))):
        for j in range(2):
            rows, contract = slice(j * width, (j + 1) * width), j
            sums = dot(near[:, 2 * j * width : (2 * j + 1) * width], own[rows], 1, contract)
            sums += dot(near[:, (2 * j + 1) * width : (2 * j + 2) * width], other[rows], 1, contract)
            parts[:, (2 * j + c) * width : (2 * j + c + 1) * width] = sums.astype(BF16)


def terms_kernel(core, both, w00, w01, w10, w11, terms, held, done):
    width = w00.shape[1]
    d = [both[:, (2 + c) * width : (3 + c) * width] for c in range(2)]
    slabs = [
        dot(d[0], row[0][:width], 1, 1) + dot(d[1], row[1][:width], 1, 1)
        for row in ((w00, w01), (w10, w11))
    ]
    for a in range(2):
        chosen = jnp.where(core[0] == a, slabs[0], slabs[1]).astype(BF16)
        held[:, :, a * width : (a + 1) * width] = chosen.reshape(4, 64, width)
    copy = pltpu.make_async_copy(held, terms, done)
    copy.start()
    copy.wait()


def two_grads(near, both, slab, column):
    width = both.shape[1] // 4
    part = lambda ref, i: ref[:, i * width : (i + 1) * width]
    return (
        dot(part(near, slab), part(both, 2 + column), 0, 0),
        dot(part(both, column), part(near, 2 + slab), 0, 0),
    )


def send_kernel(slab, column, near, both, sent):
    width = sent.shape[1]
    first, second = two_grads(near, both, slab, column)
    sent[:width] = first.astype(BF16)
    sent[width:] = second.astype(BF16)


def grads_kernel(near, both, came0, came1, came2, grad_first, grad_second):
    width = grad_first.shape[0]
    first, second = two_grads(near, both, 0, 0)
    for came in (came0, came1, came2):
        first += came[:width].astype(F32)
        second += came[width:].astype(F32)
    grad_first[...] = first
    grad_second[...] = second


def local(inputs, out_grad, w_first, w_second):
    rows, width = inputs.shape
    half = rows // 2
    core = lax.axis_index("core")

    packed = jnp.concatenate([w_first, w_second])
    held = [packed, flip(packed, 0, 1), flip(packed, 1, 0), flip(packed, 1, 1)]

    pair = jnp.stack([inputs, out_grad]).reshape(2, 2, half, width).transpose(1, 0, 2, 3)
    pair = jnp.broadcast_to(pair[None], (8, 2, 2, half, width))
    far = exchange_far(pair.reshape(16, 2, half, width)).reshape(8, 2, 2, half, width)
    far = far.transpose(2, 1, 0, 3, 4).reshape(2, 2, 8 * half, width)
    own_in, own_grad = [jnp.where(core == 0, f[0], f[1]) for f in far]
    other_in, other_grad = [jnp.where(core == 0, f[1], f[0]) for f in far]
    far = jnp.concatenate([own_in, other_in, own_grad, other_grad], axis=1)

    pieces = [lax.all_gather(far, NEAR, axis=0, tiled=True)]
    tokens = 32 * half
    near, parts = call(
        forward_kernel,
        [((tokens, 4 * width), BF16), ((tokens, 4 * width), BF16)],
        *pieces,
        *held,
    )
    parts = exchange(parts.reshape(8, tokens // 8, 4 * width), PLANE)
    (both,) = call(act_kernel, [(parts.shape, BF16)], parts, far=1)
    both = exchange(both, PLANE)
    both = both.reshape(tokens, 4 * width)

    (terms,) = call(
        terms_kernel,
        [((4, 8 * half, 2 * width), BF16)],
        core.reshape(1).astype(jnp.int32),
        both,
        *held,
        scalars=1,
        far=1,
        cost=BOUND,
    )
    ways = ((1, 1), (0, 1), (1, 0))
    sent = [
        call(
            functools.partial(send_kernel, s, c),
            [((2 * width, width), BF16)],
            near,
            both,
            cost=BOUND,
        )[0]
        for s, c in ways
    ]
    came = [flip(block, s, c) for block, (s, c) in zip(sent, ways)]
    terms = exchange(terms, NEAR)
    (terms,) = call(sum_kernel, [((8, 2, half, width), BF16)], terms, far=1)
    terms = exchange_far(terms.reshape(16, half, width)).reshape(8, 2, half, width)
    d_input = jnp.sum(terms.astype(F32), axis=0).astype(BF16).reshape(rows, width)
    grad_first, grad_second = call(grads_kernel, [((width, width), F32)] * 2, near, both, *came, cost=COST)
    return (d_input, grad_first, grad_second)


def solution(mesh):
    fine = Mesh(mesh.devices.reshape(2, 4, 2, 2, 8, 4), ("xh", "y", "core", "xl", "zh", "zl"))
    row, col = ("xh", "y", "core"), ("xl", "zh", "zl")
    placed = (P(col, row), P(col, row), P(row, col), P(col, row))
    return jax.shard_map(
        local,
        mesh=fine,
        in_specs=placed,
        out_specs=(P(col, row), P(row, col), P(col, row)),
        check_vma=False,
    )
```

time: 164 us -> 159 us (0.970)
  matrix products: 9.52 us -> 0 us
  Pallas kernels: 0 us -> 8.94 us
  blocking collectives: 45.2 us -> 50.3 us
  other arithmetic: 5.75 us -> 1.39 us
  local copies, waits for them, and re-layouts: 5.24 us -> 1.71 us
  starting transfers between devices: 83.2 us -> 80.2 us
    dot_general x20 -> x0, matrix products: 9.52 us -> none  [dot(): lax.dot_general(a, b, (((ca,), (cb,)), ((), ())), preferred_element_type=...]
    pallas_call x0 -> x8, Pallas kernels: none -> 8.94 us  [call(): pl.pallas_call(kernel, out_shape=[jax.ShapeDtypeStruct(shape, kind) for s...]
    all_to_all x2, blocking collectives: 29.8 us -> 33.6 us  [exchange(): return lax.all_to_all(blocks, axes, 0, 0, tiled=False)]
    all_to_all x2, waiting for transfers between devices: 11.2 us -> 15 us  [exchange_far(): lax.all_to_all(blocks, SPAN, 0, 0, axis_index_groups=groups, tiled=False)]
    all_to_all x2, starting transfers between devices: 61 us -> 58 us  [exchange_far(): lax.all_to_all(blocks, SPAN, 0, 0, axis_index_groups=groups, tiled=False)]
    ppermute x5 -> x6, waiting for transfers between devices: 2.46 us -> 0.02 us  [flip(): lax.ppermute(block, QUAD, [(i, i ^ 2 * slab + column) for i in range(4)])]
    concatenate x5 -> x0, other arithmetic: 1.85 us -> none  [the longest x1 0.88 us: local(): mixed = jnp.concatenate([t.astype(BF16) for t in kept[1]])]
    unnamed x9, local copies, waits for them, and re-layouts: 2.74 us -> 0.96 us
  transfers between devices with their start and end apart: 8 -> 9, of which waited for: 3 -> 2; matrix products, arithmetic and copies ran while one was open for 8% -> 0% of each run, Pallas kernels for 0% -> 4%
where the time goes in v4:
time: 159 us; the launch traced here: 158 us
  starting transfers between devices  80.2 us (50%)
  blocking collectives  50.3 us (32%)
  waiting for transfers between devices  15 us (9%)
  Pallas kernels  8.94 us (6%)
  local copies, waits for them, and re-layouts  1.71 us (1%)
    all_to_all x2, starting transfers between devices, exchange_far(): lax.all_to_all(blocks, SPAN, 0, 0, axis_index_groups=groups, tiled=False)  58 us
    all_to_all x2, blocking collectives, exchange(): return lax.all_to_all(blocks, axes, 0, 0, tiled=False)  33.6 us
    ppermute x6, starting transfers between devices, flip(): lax.ppermute(block, QUAD, [(i, i ^ 2 * slab + column) for i in range(4)])  18.5 us
    all_gather x1, blocking collectives, local(): pieces = [lax.all_gather(far, NEAR, axis=0, tiled=True)]  16.6 us
    all_to_all x2, waiting for transfers between devices, exchange_far(): lax.all_to_all(blocks, SPAN, 0, 0, axis_index_groups=groups, tiled=False)  15 us
    pallas_call x8, Pallas kernels, call(): pl.pallas_call(kernel, out_shape=[jax.ShapeDtypeStruct(shape, kind) for s...  8.94 us
    all_to_all x1, starting transfers between devices, exchange(): return lax.all_to_all(blocks, axes, 0, 0, tiled=False)  3.6 us
  transfers between devices with their start and end apart: 9, of which 2 were waited for; matrix products, arithmetic and copies ran while one was open for 0% of the time, Pallas kernels for 4%

profile of v4, /device:TPU:1, one launch (start us, length us, event | category | flops | bytes accessed | tf_op | source)
XLA Modules:
  0.0 158.3 jit_solution(2186291262944849273)
XLA Ops:
  0.6 0.7 maximum_bitcast_fusion
  1.4 0.0 copy-start.2
  1.4 0.7 broadcast_in_dim.2
  2.1 35.5 %all-to-all-start = ((bf16[16,2,8,384]{3,2,1,0:T(8,128)(2,1)}), bf16[16,2,8,384]{3,2,1,0:T(8,128)(2,1)S(1)}, u32[]{:S(2)}, u32[]{:S(2)}) async-start(bf16[16,2,8,384]{3,2,1,0:T(8,128)(2,1)} %bitcast.4), calls=%async_computation | async-start | bytes 393216 | tf_op jit(solution)/shard_map/all_to_all | solution.py:36
  37.6 0.0 copy-start.3
  37.6 0.9 copy-done.3
  38.6 3.4 %collective-permute-start.2 = (bf16[768,384]{1,0:T(8,128)(2,1)S(1)}, bf16[768,384]{1,0:T(8,128)(2,1)S(1)}, u32[]{:S(2)}, u32[]{:S(2)}) collective-permute-start(bf16[768,384]{1,0:T(8,128)(2,1)S(1)} %constant_dynamic-update-slice_fusion.refs_1_.w00), channel_id=1, source_target_pairs={{0,96},{32,64},{64,32},{96,0},{1,97},{33,65},{65,33},{97,1},{2,98}... | collective-permute-start | bytes 1769480 | tf_op jit(solution)/shard_map/ppermute | solution.py:40
  42.0 2.1 %collective-permute-start.1 = (bf16[768,384]{1,0:T(8,128)(2,1)S(1)}, bf16[768,384]{1,0:T(8,128)(2,1)S(1)}, u32[]{:S(2)}, u32[]{:S(2)}) collective-permute-start(bf16[768,384]{1,0:T(8,128)(2,1)S(1)} %constant_dynamic-update-slice_fusion.refs_1_.w00), channel_id=1, source_target_pairs={{0,64},{32,96},{64,0},{96,32},{1,65},{33,97},{65,1},{97,33},{2,66}... | collective-permute-start | bytes 1769480 | tf_op jit(solution)/shard_map/ppermute | solution.py:40
  44.1 2.2 %collective-permute-start = (bf16[768,384]{1,0:T(8,128)(2,1)S(1)}, bf16[768,384]{1,0:T(8,128)(2,1)S(1)}, u32[]{:S(2)}, u32[]{:S(2)}) collective-permute-start(bf16[768,384]{1,0:T(8,128)(2,1)S(1)} %constant_dynamic-update-slice_fusion.refs_1_.w00), channel_id=1, source_target_pairs={{0,32},{32,0},{64,96},{96,64},{1,33},{33,1},{65,97},{97,65},{2,34}... | collective-permute-start | bytes 1769480 | tf_op jit(solution)/shard_map/ppermute | solution.py:40
  46.2 8.8 %all-to-all-done = bf16[16,2,8,384]{3,2,1,0:T(8,128)(2,1)S(1)} async-done(((bf16[16,2,8,384]{3,2,1,0:T(8,128)(2,1)}), bf16[16,2,8,384]{3,2,1,0:T(8,128)(2,1)S(1)}, u32[]{:S(2)}, u32[]{:S(2)}) %all-to-all-start) | async-done | bytes 196640 | tf_op jit(solution)/shard_map/all_to_all | solution.py:36
  55.1 16.6 %all_gather.3.refs_0_ = bf16[256,1536]{1,0:T(8,128)(2,1)S(1)} all-gather(bf16[64,1536]{1,0:T(8,128)(2,1)S(1)} %pad_maximum_fusion), channel_id=1, replica_groups=mesh['xh'=2,'y'=4,'core'=2,'xl'=2,'zh'=8,'zl'=4] {'zl'}, dimensions={0}, use_global_device_ids=true | all-gather | bytes 983040 | tf_op jit(solution)/shard_map/all_gather | solution.py:165
  71.8 0.0 collective-permute-done.2.refs_4_.w11
  71.8 0.0 collective-permute-done.1.refs_3_.w10
  71.8 0.0 collective-permute-done.refs_2_.w01
  71.8 1.2 shard_map.67
  72.9 18.3 %all_to_all.25.parts = bf16[8,32,1536]{2,1,0:T(8,128)(2,1)S(1)} all-to-all(bf16[8,32,1536]{2,1,0:T(8,128)(2,1)S(1)} %bitcast.27), channel_id=1, replica_groups=mesh['xh'=2,'y'=4,'core'=2,'xl'=2,'zh'=8,'zl'=4] {'xh','y'}, dimensions={0} | all-to-all | bytes 1572864 | tf_op jit(solution)/shard_map/all_to_all | solution.py:29
  91.3 0.2 shard_map.68
  91.5 15.3 %all_to_all.26 = bf16[8,32,1536]{2,1,0:T(8,128)(2,1)S(1)} all-to-all(bf16[8,32,1536]{2,1,0:T(8,128)(2,1)S(1)} %shard_map.68), channel_id=1, replica_groups=mesh['xh'=2,'y'=4,'core'=2,'xl'=2,'zh'=8,'zl'=4] {'xh','y'}, dimensions={0} | all-to-all | bytes 1572864 | tf_op jit(solution)/shard_map/all_to_all | solution.py:29
  106.8 1.4 shard_map.69
  108.3 3.6 %all-to-all-start.3 = ((bf16[4,64,768]{2,1,0:T(8,128)(2,1)}), bf16[4,64,768]{2,1,0:T(8,128)(2,1)S(1)}, u32[]{:S(2)}, u32[]{:S(2)}) async-start(bf16[4,64,768]{2,1,0:T(8,128)(2,1)} %shard_map.69), calls=%async_computation.3 | async-start | bytes 786432 | tf_op jit(solution)/shard_map/all_to_all | solution.py:29
  111.9 0.4 shard_map.73
  112.3 1.2 shard_map.72
  113.5 1.2 shard_map.71
  114.7 6.0 %collective-permute-start.3 = (bf16[768,384]{1,0:T(8,128)(2,1)}, bf16[768,384]{1,0:T(8,128)(2,1)S(1)}, u32[]{:S(2)}, u32[]{:S(2)}) collective-permute-start(bf16[768,384]{1,0:T(8,128)(2,1)} %shard_map.71), channel_id=1, source_target_pairs={{0,96},{32,64},{64,32},{96,0},{1,97},{33,65},{65,33},{97,1},{2,98}... | collective-permute-start | bytes 1769480 | tf_op jit(solution)/shard_map/ppermute | solution.py:40
  120.7 3.0 %collective-permute-start.4 = (bf16[768,384]{1,0:T(8,128)(2,1)}, bf16[768,384]{1,0:T(8,128)(2,1)}, u32[]{:S(2)}, u32[]{:S(2)}) collective-permute-start(bf16[768,384]{1,0:T(8,128)(2,1)} %shard_map.72), channel_id=1, source_target_pairs={{0,32},{32,0},{64,96},{96,64},{1,33},{33,1},{65,97},{97,65},{2,34}... | collective-permute-start | bytes 1769480 | tf_op jit(solution)/shard_map/ppermute | solution.py:40
  123.8 1.9 %collective-permute-start.5 = (bf16[768,384]{1,0:T(8,128)(2,1)S(1)}, bf16[768,384]{1,0:T(8,128)(2,1)}, u32[]{:S(2)}, u32[]{:S(2)}) collective-permute-start(bf16[768,384]{1,0:T(8,128)(2,1)S(1)} %shard_map.73), channel_id=1, source_target_pairs={{0,64},{32,96},{64,0},{96,32},{1,65},{33,97},{65,1},{97,33},{2,66}... | collective-permute-start | bytes 1769480 | tf_op jit(solution)/shard_map/ppermute | solution.py:40
  125.7 0.7 shard_map.70
  126.4 22.5 %all-to-all-start.4 = ((bf16[16,8,384]{2,1,0:T(8,128)(2,1)}), bf16[16,8,384]{2,1,0:T(8,128)(2,1)S(1)}, u32[]{:S(2)}, u32[]{:S(2)}) async-start(bf16[16,8,384]{2,1,0:T(8,128)(2,1)} %bitcast.14), calls=%async_computation.4 | async-start | bytes 196608 | tf_op jit(solution)/shard_map/all_to_all | solution.py:36
  149.0 0.0 collective-permute-done.4.came1
  149.0 2.6 %shard_map.74 = (f32[384,384]{1,0:T(8,128)}, f32[384,384]{1,0:T(8,128)}) custom-call(bf16[256,1536]{1,0:T(8,128)(2,1)S(1)} %copy-done.1, bf16[256,1536]{1,0:T(8,128)(2,1)S(1)} %bitcast.26, bf16[768,384]{1,0:T(8,128)(2,1)S(1)} %collective-permute-done.3.came0, bf16[768,384]{1,0:T(8,128)(2,1)} %collective-permute-done.4.came1, ...), custom_call_target="tpu_custom_call" | custom-call | flops 30000001024 | bytes 4194304 | tf_op jit(solution)/shard_map/pallas_call | solution.py:54
  151.6 6.1 %all-to-all-done.4 = bf16[16,8,384]{2,1,0:T(8,128)(2,1)S(1)} async-done(((bf16[16,8,384]{2,1,0:T(8,128)(2,1)}), bf16[16,8,384]{2,1,0:T(8,128)(2,1)S(1)}, u32[]{:S(2)}, u32[]{:S(2)}) %all-to-all-start.4) | async-done | bytes 98336 | tf_op jit(solution)/shard_map/all_to_all | solution.py:36
  157.7 0.6 reduce_sum.12
  (13 shorter events, 0.1 us)
Async XLA Ops:
  1.4 36.2 %copy-start.2 = (bf16[384,384]{1,0:T(8,128)(2,1)S(1)}, bf16[384,384]{1,0:T(8,128)(2,1)}, u32[]{:S(2)}) copy-start(bf16[384,384]{1,0:T(8,128)(2,1)} %param.6) | copy-start | bytes 884740
  2.1 53.0 %all-to-all-start = ((bf16[16,2,8,384]{3,2,1,0:T(8,128)(2,1)}), bf16[16,2,8,384]{3,2,1,0:T(8,128)(2,1)S(1)}, u32[]{:S(2)}, u32[]{:S(2)}) async-start(bf16[16,2,8,384]{3,2,1,0:T(8,128)(2,1)} %bitcast.4), calls=%async_computation | async-start | bytes 393216 | tf_op jit(solution)/shard_map/all_to_all | solution.py:36
  37.6 1.0 copy-start.3
  38.6 33.1 %collective-permute-start.2 = (bf16[768,384]{1,0:T(8,128)(2,1)S(1)}, bf16[768,384]{1,0:T(8,128)(2,1)S(1)}, u32[]{:S(2)}, u32[]{:S(2)}) collective-permute-start(bf16[768,384]{1,0:T(8,128)(2,1)S(1)} %constant_dynamic-update-slice_fusion.refs_1_.w00), channel_id=1, source_target_pairs={{0,96},{32,64},{64,32},{96,0},{1,97},{33,65},{65,33},{97,1},{2,98}... | collective-permute-start | bytes 1769480 | tf_op jit(solution)/shard_map/ppermute | solution.py:40
  42.0 29.8 %collective-permute-start.1 = (bf16[768,384]{1,0:T(8,128)(2,1)S(1)}, bf16[768,384]{1,0:T(8,128)(2,1)S(1)}, u32[]{:S(2)}, u32[]{:S(2)}) collective-permute-start(bf16[768,384]{1,0:T(8,128)(2,1)S(1)} %constant_dynamic-update-slice_fusion.refs_1_.w00), channel_id=1, source_target_pairs={{0,64},{32,96},{64,0},{96,32},{1,65},{33,97},{65,1},{97,33},{2,66}... | collective-permute-start | bytes 1769480 | tf_op jit(solution)/shard_map/ppermute | solution.py:40
  44.1 27.7 %collective-permute-start = (bf16[768,384]{1,0:T(8,128)(2,1)S(1)}, bf16[768,384]{1,0:T(8,128)(2,1)S(1)}, u32[]{:S(2)}, u32[]{:S(2)}) collective-permute-start(bf16[768,384]{1,0:T(8,128)(2,1)S(1)} %constant_dynamic-update-slice_fusion.refs_1_.w00), channel_id=1, source_target_pairs={{0,32},{32,0},{64,96},{96,64},{1,33},{33,1},{65,97},{97,65},{2,34}... | collective-permute-start | bytes 1769480 | tf_op jit(solution)/shard_map/ppermute | solution.py:40
  72.9 18.3 %copy-start = (bf16[256,1536]{1,0:T(8,128)(2,1)}, bf16[256,1536]{1,0:T(8,128)(2,1)S(1)}, u32[]{:S(2)}) copy-start(bf16[256,1536]{1,0:T(8,128)(2,1)S(1)} %get-tuple-element.8.near) | copy-start | bytes 2359300
  108.3 3.6 %copy-start.1 = (bf16[256,1536]{1,0:T(8,128)(2,1)S(1)}, bf16[256,1536]{1,0:T(8,128)(2,1)}, u32[]{:S(2)}) copy-start(bf16[256,1536]{1,0:T(8,128)(2,1)} %copy-done) | copy-start | bytes 2359300
  108.3 17.4 %all-to-all-start.3 = ((bf16[4,64,768]{2,1,0:T(8,128)(2,1)}), bf16[4,64,768]{2,1,0:T(8,128)(2,1)S(1)}, u32[]{:S(2)}, u32[]{:S(2)}) async-start(bf16[4,64,768]{2,1,0:T(8,128)(2,1)} %shard_map.69), calls=%async_computation.3 | async-start | bytes 786432 | tf_op jit(solution)/shard_map/all_to_all | solution.py:29
  114.7 34.2 %collective-permute-start.3 = (bf16[768,384]{1,0:T(8,128)(2,1)}, bf16[768,384]{1,0:T(8,128)(2,1)S(1)}, u32[]{:S(2)}, u32[]{:S(2)}) collective-permute-start(bf16[768,384]{1,0:T(8,128)(2,1)} %shard_map.71), channel_id=1, source_target_pairs={{0,96},{32,64},{64,32},{96,0},{1,97},{33,65},{65,33},{97,1},{2,98}... | collective-permute-start | bytes 1769480 | tf_op jit(solution)/shard_map/ppermute | solution.py:40
  120.7 28.2 %collective-permute-start.4 = (bf16[768,384]{1,0:T(8,128)(2,1)}, bf16[768,384]{1,0:T(8,128)(2,1)}, u32[]{:S(2)}, u32[]{:S(2)}) collective-permute-start(bf16[768,384]{1,0:T(8,128)(2,1)} %shard_map.72), channel_id=1, source_target_pairs={{0,32},{32,0},{64,96},{96,64},{1,33},{33,1},{65,97},{97,65},{2,34}... | collective-permute-start | bytes 1769480 | tf_op jit(solution)/shard_map/ppermute | solution.py:40
  123.8 25.2 %collective-permute-start.5 = (bf16[768,384]{1,0:T(8,128)(2,1)S(1)}, bf16[768,384]{1,0:T(8,128)(2,1)}, u32[]{:S(2)}, u32[]{:S(2)}) collective-permute-start(bf16[768,384]{1,0:T(8,128)(2,1)S(1)} %shard_map.73), channel_id=1, source_target_pairs={{0,64},{32,96},{64,0},{96,32},{1,65},{33,97},{65,1},{97,33},{2,66}... | collective-permute-start | bytes 1769480 | tf_op jit(solution)/shard_map/ppermute | solution.py:40
  126.4 31.3 %all-to-all-start.4 = ((bf16[16,8,384]{2,1,0:T(8,128)(2,1)}), bf16[16,8,384]{2,1,0:T(8,128)(2,1)S(1)}, u32[]{:S(2)}, u32[]{:S(2)}) async-start(bf16[16,8,384]{2,1,0:T(8,128)(2,1)} %bitcast.14), calls=%async_computation.4 | async-start | bytes 196608 | tf_op jit(solution)/shard_map/all_to_all | solution.py:36

commit v5 on v4

--- a/solution.py
+++ b/solution.py
@@ -1,4 +1,3 @@
-import functools
 import math
 
 import jax
@@ -15,6 +14,7 @@
 BOUND = pl.CostEstimate(flops=10**9, bytes_accessed=2**10, transcendentals=0)
 SPAN = ("core", "zh", "zl")
 NEAR = ("zl",)
+WAYS = ((1, 1), (0, 1), (1, 0))
 F32 = jnp.float32
 BF16 = jnp.bfloat16
 
@@ -44,7 +44,7 @@
     return lax.dot_general(a, b, (((ca,), (cb,)), ((), ())), preferred_element_type=F32)
 
 
-def call(kernel, outs, *operands, scalars=0, far=0, cost=None):
+def call(kernel, outs, *operands, scalars=0, far=0, cost=None, limit=LIMIT):
     specs = [pl.BlockSpec(memory_space=pltpu.SMEM)] * scalars
     specs += [pl.BlockSpec(memory_space=pltpu.VMEM)] * (len(operands) - scalars)
     out_specs = [pl.BlockSpec(memory_space=pltpu.HBM)] * far
@@ -58,8 +58,21 @@
         out_specs=out_specs,
         scratch_shapes=scratch,
         cost_estimate=cost,
-        compiler_params=pltpu.CompilerParams(vmem_limit_bytes=LIMIT * 2**20),
+        compiler_params=pltpu.CompilerParams(vmem_limit_bytes=limit * 2**20),
     )(*operands)
+
+
+def spread_kernel(inputs, out_grad, out, held, done):
+    half = inputs.shape[0] // 2
+    for i, block in enumerate((inputs, out_grad)):
+        wide = block[...].astype(F32)
+        for c in range(2):
+            piece = wide[c * half : (c + 1) * half].astype(BF16)
+            for k in range(8):
+                held[k, c, i] = piece
+    copy = pltpu.make_async_copy(held, out, done)
+    copy.start()
+    copy.wait()
 
 
 def act_kernel(parts, out, held, done):
@@ -129,11 +142,19 @@
     )
 
 
-def send_kernel(slab, column, near, both, sent):
-    width = sent.shape[1]
-    first, second = two_grads(near, both, slab, column)
-    sent[:width] = first.astype(BF16)
-    sent[width:] = second.astype(BF16)
+def send_kernel(near, both, out0, out1, out2, held0, held1, held2, done0, done1, done2):
+    width = out0.shape[1]
+    copies = []
+    for (slab, column), out, held, done in zip(
+        WAYS, (out0, out1, out2), (held0, held1, held2), (done0, done1, done2)
+    ):
+        first, second = two_grads(near, both, slab, column)
+        held[:width] = first.astype(BF16)
+        held[width:] = second.astype(BF16)
+        copies.append(pltpu.make_async_copy(held, out, done))
+        copies[-1].start()
+    for copy in copies:
+        copy.wait()
 
 
 def grads_kernel(near, both, came0, came1, came2, grad_first, grad_second):
@@ -154,8 +175,8 @@
     packed = jnp.concatenate([w_first, w_second])
     held = [packed, flip(packed, 0, 1), flip(packed, 1, 0), flip(packed, 1, 1)]
 
-    pair = jnp.stack([inputs, out_grad]).reshape(2, 2, half, width).transpose(1, 0, 2, 3)
-    pair = jnp.broadcast_to(pair[None], (8, 2, 2, half, width))
+    blocks = [((8, 2, 2, half, width), BF16)]
+    (pair,) = call(spread_kernel, blocks, inputs, out_grad, far=1, limit=56)
     far = exchange_far(pair.reshape(16, 2, half, width)).reshape(8, 2, 2, half, width)
     far = far.transpose(2, 1, 0, 3, 4).reshape(2, 2, 8 * half, width)
     own_in, own_grad = [jnp.where(core == 0, f[0], f[1]) for f in far]
@@ -185,18 +206,9 @@
         far=1,
         cost=BOUND,
     )
-    ways = ((1, 1), (0, 1), (1, 0))
-    sent = [
-        call(
-            functools.partial(send_kernel, s, c),
-            [((2 * width, width), BF16)],
-            near,
-            both,
-            cost=BOUND,
-        )[0]
-        for s, c in ways
-    ]
-    came = [flip(block, s, c) for block, (s, c) in zip(sent, ways)]
+    blocks = [((2 * width, width), BF16)] * 3
+    sent = call(send_kernel, blocks, near, both, far=3, cost=BOUND)
+    came = [flip(block, *way) for block, way in zip(sent, WAYS)]
     terms = exchange(terms, NEAR)
     (terms,) = call(sum_kernel, [((8, 2, half, width), BF16)], terms, far=1)
     terms = exchange_far(terms.reshape(16, half, width)).reshape(8, 2, half, width)

time: 159 us -> 158 us (level)
    pallas_call x8 -> x7, Pallas kernels: 8.94 us -> 9.17 us  [call(): pl.pallas_call(kernel, out_shape=[jax.ShapeDtypeStruct(shape, kind) for s...]
  transfers between devices with their start and end apart: 9 -> 9, of which waited for: 2 -> 2; matrix products, arithmetic and copies ran while one was open for 0% -> 0% of each run, Pallas kernels for 4% -> 3%
where the time goes in v5:
time: 158 us; the launch traced here: 157 us
  starting transfers between devices  80.2 us (51%)
  blocking collectives  50.3 us (32%)
  waiting for transfers between devices  15.2 us (10%)
  Pallas kernels  9.17 us (6%)
    all_to_all x2, starting transfers between devices, exchange_far(): lax.all_to_all(blocks, SPAN, 0, 0, axis_index_groups=groups, tiled=False)  58.1 us
    all_to_all x2, blocking collectives, exchange(): return lax.all_to_all(blocks, axes, 0, 0, tiled=False)  33.6 us
    ppermute x6, starting transfers between devices, flip(): lax.ppermute(block, QUAD, [(i, i ^ 2 * slab + column) for i in range(4)])  18.5 us
    all_gather x1, blocking collectives, local(): pieces = [lax.all_gather(far, NEAR, axis=0, tiled=True)]  16.6 us
    all_to_all x2, waiting for transfers between devices, exchange_far(): lax.all_to_all(blocks, SPAN, 0, 0, axis_index_groups=groups, tiled=False)  15.2 us
    pallas_call x7, Pallas kernels, call(): pl.pallas_call(kernel, out_shape=[jax.ShapeDtypeStruct(shape, kind) for s...  9.17 us
    all_to_all x1, starting transfers between devices, exchange(): return lax.all_to_all(blocks, axes, 0, 0, tiled=False)  3.6 us
  transfers between devices with their start and end apart: 9, of which 2 were waited for; matrix products, arithmetic and copies ran while one was open for 0% of the time, Pallas kernels for 3%

profile of v5, /device:TPU:1, one launch (start us, length us, event | category | flops | bytes accessed | tf_op | source)
XLA Modules:
  0.0 157.3 jit_solution(2936451177447403926)
XLA Ops:
  0.6 0.0 copy-start.2
  0.6 1.5 shard_map.67
  2.1 35.5 %all-to-all-start = ((bf16[16,2,8,384]{3,2,1,0:T(8,128)(2,1)}), bf16[16,2,8,384]{3,2,1,0:T(8,128)(2,1)S(1)}, u32[]{:S(2)}, u32[]{:S(2)}) async-start(bf16[16,2,8,384]{3,2,1,0:T(8,128)(2,1)} %bitcast.23), calls=%async_computation | async-start | bytes 393216 | tf_op jit(solution)/shard_map/all_to_all | solution.py:36
  37.7 0.0 copy-start.3
  37.7 0.9 copy-done.3
  38.7 3.4 %collective-permute-start.2 = (bf16[768,384]{1,0:T(8,128)(2,1)S(1)}, bf16[768,384]{1,0:T(8,128)(2,1)S(1)}, u32[]{:S(2)}, u32[]{:S(2)}) collective-permute-start(bf16[768,384]{1,0:T(8,128)(2,1)S(1)} %constant_dynamic-update-slice_fusion.refs_1_.w00), channel_id=1, source_target_pairs={{0,96},{32,64},{64,32},{96,0},{1,97},{33,65},{65,33},{97,1},{2,98}... | collective-permute-start | bytes 1769480 | tf_op jit(solution)/shard_map/ppermute | solution.py:40
  42.0 2.1 %collective-permute-start.1 = (bf16[768,384]{1,0:T(8,128)(2,1)S(1)}, bf16[768,384]{1,0:T(8,128)(2,1)S(1)}, u32[]{:S(2)}, u32[]{:S(2)}) collective-permute-start(bf16[768,384]{1,0:T(8,128)(2,1)S(1)} %constant_dynamic-update-slice_fusion.refs_1_.w00), channel_id=1, source_target_pairs={{0,64},{32,96},{64,0},{96,32},{1,65},{33,97},{65,1},{97,33},{2,66}... | collective-permute-start | bytes 1769480 | tf_op jit(solution)/shard_map/ppermute | solution.py:40
  44.1 2.2 %collective-permute-start = (bf16[768,384]{1,0:T(8,128)(2,1)S(1)}, bf16[768,384]{1,0:T(8,128)(2,1)S(1)}, u32[]{:S(2)}, u32[]{:S(2)}) collective-permute-start(bf16[768,384]{1,0:T(8,128)(2,1)S(1)} %constant_dynamic-update-slice_fusion.refs_1_.w00), channel_id=1, source_target_pairs={{0,32},{32,0},{64,96},{96,64},{1,33},{33,1},{65,97},{97,65},{2,34}... | collective-permute-start | bytes 1769480 | tf_op jit(solution)/shard_map/ppermute | solution.py:40
  46.3 8.8 %all-to-all-done = bf16[16,2,8,384]{3,2,1,0:T(8,128)(2,1)S(1)} async-done(((bf16[16,2,8,384]{3,2,1,0:T(8,128)(2,1)}), bf16[16,2,8,384]{3,2,1,0:T(8,128)(2,1)S(1)}, u32[]{:S(2)}, u32[]{:S(2)}) %all-to-all-start) | async-done | bytes 196640 | tf_op jit(solution)/shard_map/all_to_all | solution.py:36
  55.2 16.6 %all_gather.3.refs_0_ = bf16[256,1536]{1,0:T(8,128)(2,1)S(1)} all-gather(bf16[64,1536]{1,0:T(8,128)(2,1)S(1)} %pad_maximum_fusion), channel_id=1, replica_groups=mesh['xh'=2,'y'=4,'core'=2,'xl'=2,'zh'=8,'zl'=4] {'zl'}, dimensions={0}, use_global_device_ids=true | all-gather | bytes 983040 | tf_op jit(solution)/shard_map/all_gather | solution.py:186
  71.8 0.0 collective-permute-done.2.refs_4_.w11
  71.8 0.0 collective-permute-done.1.refs_3_.w10
  71.8 0.0 collective-permute-done.refs_2_.w01
  71.8 1.2 shard_map.68
  73.0 18.3 %all_to_all.25.parts = bf16[8,32,1536]{2,1,0:T(8,128)(2,1)S(1)} all-to-all(bf16[8,32,1536]{2,1,0:T(8,128)(2,1)S(1)} %bitcast.21), channel_id=1, replica_groups=mesh['xh'=2,'y'=4,'core'=2,'xl'=2,'zh'=8,'zl'=4] {'xh','y'}, dimensions={0} | all-to-all | bytes 1572864 | tf_op jit(solution)/shard_map/all_to_all | solution.py:29
  91.3 0.2 shard_map.69
  91.6 15.3 %all_to_all.26 = bf16[8,32,1536]{2,1,0:T(8,128)(2,1)S(1)} all-to-all(bf16[8,32,1536]{2,1,0:T(8,128)(2,1)S(1)} %shard_map.69), channel_id=1, replica_groups=mesh['xh'=2,'y'=4,'core'=2,'xl'=2,'zh'=8,'zl'=4] {'xh','y'}, dimensions={0} | all-to-all | bytes 1572864 | tf_op jit(solution)/shard_map/all_to_all | solution.py:29
  106.9 1.4 shard_map.70
  108.3 3.6 %all-to-all-start.3 = ((bf16[4,64,768]{2,1,0:T(8,128)(2,1)}), bf16[4,64,768]{2,1,0:T(8,128)(2,1)S(1)}, u32[]{:S(2)}, u32[]{:S(2)}) async-start(bf16[4,64,768]{2,1,0:T(8,128)(2,1)} %shard_map.70), calls=%async_computation.3 | async-start | bytes 786432 | tf_op jit(solution)/shard_map/all_to_all | solution.py:29
  111.9 1.8 %shard_map.72 = (bf16[768,384]{1,0:T(8,128)(2,1)}, bf16[768,384]{1,0:T(8,128)(2,1)}, bf16[768,384]{1,0:T(8,128)(2,1)}) custom-call(bf16[256,1536]{1,0:T(8,128)(2,1)S(1)} %copy-done.1, bf16[256,1536]{1,0:T(8,128)(2,1)S(1)} %bitcast.19), custom_call_target="tpu_custom_call" | custom-call | flops 1000000000 | bytes 1024 | tf_op jit(solution)/shard_map/pallas_call | solution.py:54
  113.7 6.0 %collective-permute-start.3 = (bf16[768,384]{1,0:T(8,128)(2,1)}, bf16[768,384]{1,0:T(8,128)(2,1)S(1)}, u32[]{:S(2)}, u32[]{:S(2)}) collective-permute-start(bf16[768,384]{1,0:T(8,128)(2,1)} %get-tuple-element.12), channel_id=1, source_target_pairs={{0,96},{32,64},{64,32},{96,0},{1,97},{33,65},{65,33},{97,1},{2,98}... | collective-permute-start | bytes 1769480 | tf_op jit(solution)/shard_map/ppermute | solution.py:40
  119.7 3.0 %collective-permute-start.4 = (bf16[768,384]{1,0:T(8,128)(2,1)}, bf16[768,384]{1,0:T(8,128)(2,1)S(1)}, u32[]{:S(2)}, u32[]{:S(2)}) collective-permute-start(bf16[768,384]{1,0:T(8,128)(2,1)} %get-tuple-element.13), channel_id=1, source_target_pairs={{0,32},{32,0},{64,96},{96,64},{1,33},{33,1},{65,97},{97,65},{2,34}... | collective-permute-start | bytes 1769480 | tf_op jit(solution)/shard_map/ppermute | solution.py:40
  122.8 1.9 %collective-permute-start.5 = (bf16[768,384]{1,0:T(8,128)(2,1)}, bf16[768,384]{1,0:T(8,128)(2,1)}, u32[]{:S(2)}, u32[]{:S(2)}) collective-permute-start(bf16[768,384]{1,0:T(8,128)(2,1)} %get-tuple-element.14), channel_id=1, source_target_pairs={{0,64},{32,96},{64,0},{96,32},{1,65},{33,97},{65,1},{97,33},{2,66}... | collective-permute-start | bytes 1769480 | tf_op jit(solution)/shard_map/ppermute | solution.py:40
  124.7 0.0 all-to-all-done.3.terms
  124.7 0.7 shard_map.71
  125.4 22.6 %all-to-all-start.4 = ((bf16[16,8,384]{2,1,0:T(8,128)(2,1)}), bf16[16,8,384]{2,1,0:T(8,128)(2,1)S(1)}, u32[]{:S(2)}, u32[]{:S(2)}) async-start(bf16[16,8,384]{2,1,0:T(8,128)(2,1)} %bitcast.11), calls=%async_computation.4 | async-start | bytes 196608 | tf_op jit(solution)/shard_map/all_to_all | solution.py:36
  148.0 0.0 collective-permute-done.3.came0
  148.0 0.0 collective-permute-done.4.came1
  148.0 0.0 collective-permute-done.5.came2
  148.0 2.4 %shard_map.73 = (f32[384,384]{1,0:T(8,128)}, f32[384,384]{1,0:T(8,128)}) custom-call(bf16[256,1536]{1,0:T(8,128)(2,1)S(1)} %copy-done.1, bf16[256,1536]{1,0:T(8,128)(2,1)S(1)} %bitcast.20, bf16[768,384]{1,0:T(8,128)(2,1)S(1)} %collective-permute-done.3.came0, bf16[768,384]{1,0:T(8,128)(2,1)S(1)} %collective-permute-done.4.came1, ...), custom_call_target="tpu_custom_call" | custom-call | flops 30000001024 | bytes 4194304 | tf_op jit(solution)/shard_map/pallas_call | solution.py:54
  150.4 6.3 %all-to-all-done.4 = bf16[16,8,384]{2,1,0:T(8,128)(2,1)S(1)} async-done(((bf16[16,8,384]{2,1,0:T(8,128)(2,1)}), bf16[16,8,384]{2,1,0:T(8,128)(2,1)S(1)}, u32[]{:S(2)}, u32[]{:S(2)}) %all-to-all-start.4) | async-done | bytes 98336 | tf_op jit(solution)/shard_map/all_to_all | solution.py:36
  156.7 0.6 reduce_sum.12
  (9 shorter events, 0.1 us)
Async XLA Ops:
  0.6 37.0 %copy-start.2 = (bf16[384,384]{1,0:T(8,128)(2,1)S(1)}, bf16[384,384]{1,0:T(8,128)(2,1)}, u32[]{:S(2)}) copy-start(bf16[384,384]{1,0:T(8,128)(2,1)} %param.6) | copy-start | bytes 884740
  2.1 53.0 %all-to-all-start = ((bf16[16,2,8,384]{3,2,1,0:T(8,128)(2,1)}), bf16[16,2,8,384]{3,2,1,0:T(8,128)(2,1)S(1)}, u32[]{:S(2)}, u32[]{:S(2)}) async-start(bf16[16,2,8,384]{3,2,1,0:T(8,128)(2,1)} %bitcast.23), calls=%async_computation | async-start | bytes 393216 | tf_op jit(solution)/shard_map/all_to_all | solution.py:36
  37.7 1.0 copy-start.3
  38.7 33.1 %collective-permute-start.2 = (bf16[768,384]{1,0:T(8,128)(2,1)S(1)}, bf16[768,384]{1,0:T(8,128)(2,1)S(1)}, u32[]{:S(2)}, u32[]{:S(2)}) collective-permute-start(bf16[768,384]{1,0:T(8,128)(2,1)S(1)} %constant_dynamic-update-slice_fusion.refs_1_.w00), channel_id=1, source_target_pairs={{0,96},{32,64},{64,32},{96,0},{1,97},{33,65},{65,33},{97,1},{2,98}... | collective-permute-start | bytes 1769480 | tf_op jit(solution)/shard_map/ppermute | solution.py:40
  42.0 29.8 %collective-permute-start.1 = (bf16[768,384]{1,0:T(8,128)(2,1)S(1)}, bf16[768,384]{1,0:T(8,128)(2,1)S(1)}, u32[]{:S(2)}, u32[]{:S(2)}) collective-permute-start(bf16[768,384]{1,0:T(8,128)(2,1)S(1)} %constant_dynamic-update-slice_fusion.refs_1_.w00), channel_id=1, source_target_pairs={{0,64},{32,96},{64,0},{96,32},{1,65},{33,97},{65,1},{97,33},{2,66}... | collective-permute-start | bytes 1769480 | tf_op jit(solution)/shard_map/ppermute | solution.py:40
  44.1 27.7 %collective-permute-start = (bf16[768,384]{1,0:T(8,128)(2,1)S(1)}, bf16[768,384]{1,0:T(8,128)(2,1)S(1)}, u32[]{:S(2)}, u32[]{:S(2)}) collective-permute-start(bf16[768,384]{1,0:T(8,128)(2,1)S(1)} %constant_dynamic-update-slice_fusion.refs_1_.w00), channel_id=1, source_target_pairs={{0,32},{32,0},{64,96},{96,64},{1,33},{33,1},{65,97},{97,65},{2,34}... | collective-permute-start | bytes 1769480 | tf_op jit(solution)/shard_map/ppermute | solution.py:40
  73.0 18.3 %copy-start = (bf16[256,1536]{1,0:T(8,128)(2,1)}, bf16[256,1536]{1,0:T(8,128)(2,1)S(1)}, u32[]{:S(2)}) copy-start(bf16[256,1536]{1,0:T(8,128)(2,1)S(1)} %get-tuple-element.11.near) | copy-start | bytes 2359300
  108.3 3.6 %copy-start.1 = (bf16[256,1536]{1,0:T(8,128)(2,1)S(1)}, bf16[256,1536]{1,0:T(8,128)(2,1)}, u32[]{:S(2)}) copy-start(bf16[256,1536]{1,0:T(8,128)(2,1)} %copy-done) | copy-start | bytes 2359300
  108.3 16.4 %all-to-all-start.3 = ((bf16[4,64,768]{2,1,0:T(8,128)(2,1)}), bf16[4,64,768]{2,1,0:T(8,128)(2,1)S(1)}, u32[]{:S(2)}, u32[]{:S(2)}) async-start(bf16[4,64,768]{2,1,0:T(8,128)(2,1)} %shard_map.70), calls=%async_computation.3 | async-start | bytes 786432 | tf_op jit(solution)/shard_map/all_to_all | solution.py:29
  113.7 34.3 %collective-permute-start.3 = (bf16[768,384]{1,0:T(8,128)(2,1)}, bf16[768,384]{1,0:T(8,128)(2,1)S(1)}, u32[]{:S(2)}, u32[]{:S(2)}) collective-permute-start(bf16[768,384]{1,0:T(8,128)(2,1)} %get-tuple-element.12), channel_id=1, source_target_pairs={{0,96},{32,64},{64,32},{96,0},{1,97},{33,65},{65,33},{97,1},{2,98}... | collective-permute-start | bytes 1769480 | tf_op jit(solution)/shard_map/ppermute | solution.py:40
  119.7 28.2 %collective-permute-start.4 = (bf16[768,384]{1,0:T(8,128)(2,1)}, bf16[768,384]{1,0:T(8,128)(2,1)S(1)}, u32[]{:S(2)}, u32[]{:S(2)}) collective-permute-start(bf16[768,384]{1,0:T(8,128)(2,1)} %get-tuple-element.13), channel_id=1, source_target_pairs={{0,32},{32,0},{64,96},{96,64},{1,33},{33,1},{65,97},{97,65},{2,34}... | collective-permute-start | bytes 1769480 | tf_op jit(solution)/shard_map/ppermute | solution.py:40
  122.8 25.2 %collective-permute-start.5 = (bf16[768,384]{1,0:T(8,128)(2,1)}, bf16[768,384]{1,0:T(8,128)(2,1)}, u32[]{:S(2)}, u32[]{:S(2)}) collective-permute-start(bf16[768,384]{1,0:T(8,128)(2,1)} %get-tuple-element.14), channel_id=1, source_target_pairs={{0,64},{32,96},{64,0},{96,32},{1,65},{33,97},{65,1},{97,33},{2,66}... | collective-permute-start | bytes 1769480 | tf_op jit(solution)/shard_map/ppermute | solution.py:40
  125.4 31.3 %all-to-all-start.4 = ((bf16[16,8,384]{2,1,0:T(8,128)(2,1)}), bf16[16,8,384]{2,1,0:T(8,128)(2,1)S(1)}, u32[]{:S(2)}, u32[]{:S(2)}) async-start(bf16[16,8,384]{2,1,0:T(8,128)(2,1)} %bitcast.11), calls=%async_computation.4 | async-start | bytes 196608 | tf_op jit(solution)/shard_map/all_to_all | solution.py:36

commit v6 on v5

--- a/solution.py
+++ b/solution.py
@@ -13,7 +13,8 @@
 COST = pl.CostEstimate(flops=30 * 10**9, bytes_accessed=2**22, transcendentals=0)
 BOUND = pl.CostEstimate(flops=10**9, bytes_accessed=2**10, transcendentals=0)
 SPAN = ("core", "zh", "zl")
-NEAR = ("zl",)
+RING = ("zh", "zl")
+FOLD = [[z * 4 + low for low in (1, 0, 2, 3)] for z in range(8)]
 WAYS = ((1, 1), (0, 1), (1, 0))
 F32 = jnp.float32
 BF16 = jnp.bfloat16
@@ -183,7 +184,7 @@
     other_in, other_grad = [jnp.where(core == 0, f[1], f[0]) for f in far]
     far = jnp.concatenate([own_in, other_in, own_grad, other_grad], axis=1)
 
-    pieces = [lax.all_gather(far, NEAR, axis=0, tiled=True)]
+    pieces = [lax.all_gather(far, RING, axis=0, axis_index_groups=FOLD, tiled=True)]
     tokens = 32 * half
     near, parts = call(
         forward_kernel,
@@ -209,7 +210,7 @@
     blocks = [((2 * width, width), BF16)] * 3
     sent = call(send_kernel, blocks, near, both, far=3, cost=BOUND)
     came = [flip(block, *way) for block, way in zip(sent, WAYS)]
-    terms = exchange(terms, NEAR)
+    terms = lax.all_to_all(terms, RING, 0, 0, axis_index_groups=FOLD, tiled=False)
     (terms,) = call(sum_kernel, [((8, 2, half, width), BF16)], terms, far=1)
     terms = exchange_far(terms.reshape(16, half, width)).reshape(8, 2, half, width)
     d_input = jnp.sum(terms.astype(F32), axis=0).astype(BF16).reshape(rows, width)

time: 158 us -> 157 us (level)
    all_to_all x2, blocking collectives: 33.6 us -> 35.3 us  [exchange(): return lax.all_to_all(blocks, axes, 0, 0, tiled=False)]
where the time goes in v6:
time: 157 us
  starting transfers between devices  78.8 us (50%)
  blocking collectives  51.7 us (33%)
  waiting for transfers between devices  14.4 us (9%)
  Pallas kernels  9.17 us (6%)
    all_to_all x2, starting transfers between devices, exchange_far(): lax.all_to_all(blocks, SPAN, 0, 0, axis_index_groups=groups, tiled=False)  57.3 us
    all_to_all x2, blocking collectives, exchange(): return lax.all_to_all(blocks, axes, 0, 0, tiled=False)  35.3 us
    ppermute x6, starting transfers between devices, flip(): lax.ppermute(block, QUAD, [(i, i ^ 2 * slab + column) for i in range(4)])  17.9 us
    all_gather x1, blocking collectives, local(): lax.all_gather(far, RING, axis=0, axis_index_groups=FOLD, tiled=True)  16.4 us
    all_to_all x2, waiting for transfers between devices, exchange_far(): lax.all_to_all(blocks, SPAN, 0, 0, axis_index_groups=groups, tiled=False)  14.4 us
    pallas_call x7, Pallas kernels, call(): pl.pallas_call(kernel, out_shape=[jax.ShapeDtypeStruct(shape, kind) for s...  9.17 us
    all_to_all x1, starting transfers between devices, local(): lax.all_to_all(terms, RING, 0, 0, axis_index_groups=FOLD, tiled=False)  3.59 us
  transfers between devices with their start and end apart: 9, of which 2 were waited for; matrix products, arithmetic and copies ran while one was open for 0% of the time, Pallas kernels for 3%

profile of v6, /device:TPU:1, one launch (start us, length us, event | category | flops | bytes accessed | tf_op | source)
XLA Modules:
  0.0 156.6 jit_solution(14409078455855269764)
XLA Ops:
  0.6 0.0 copy-start.2
  0.6 1.5 shard_map.67
  2.1 35.5 %all-to-all-start = ((bf16[16,2,8,384]{3,2,1,0:T(8,128)(2,1)}), bf16[16,2,8,384]{3,2,1,0:T(8,128)(2,1)S(1)}, u32[]{:S(2)}, u32[]{:S(2)}) async-start(bf16[16,2,8,384]{3,2,1,0:T(8,128)(2,1)} %bitcast.23), calls=%async_computation | async-start | bytes 393216 | tf_op jit(solution)/shard_map/all_to_all | solution.py:37
  37.7 0.0 copy-start.3
  37.7 0.9 copy-done.3
  38.7 3.4 %collective-permute-start.2 = (bf16[768,384]{1,0:T(8,128)(2,1)S(1)}, bf16[768,384]{1,0:T(8,128)(2,1)S(1)}, u32[]{:S(2)}, u32[]{:S(2)}) collective-permute-start(bf16[768,384]{1,0:T(8,128)(2,1)S(1)} %constant_dynamic-update-slice_fusion.refs_1_.w00), channel_id=1, source_target_pairs={{0,96},{32,64},{64,32},{96,0},{1,97},{33,65},{65,33},{97,1},{2,98}... | collective-permute-start | bytes 1769480 | tf_op jit(solution)/shard_map/ppermute | solution.py:41
  42.0 2.1 %collective-permute-start.1 = (bf16[768,384]{1,0:T(8,128)(2,1)S(1)}, bf16[768,384]{1,0:T(8,128)(2,1)S(1)}, u32[]{:S(2)}, u32[]{:S(2)}) collective-permute-start(bf16[768,384]{1,0:T(8,128)(2,1)S(1)} %constant_dynamic-update-slice_fusion.refs_1_.w00), channel_id=1, source_target_pairs={{0,64},{32,96},{64,0},{96,32},{1,65},{33,97},{65,1},{97,33},{2,66}... | collective-permute-start | bytes 1769480 | tf_op jit(solution)/shard_map/ppermute | solution.py:41
  44.1 2.2 %collective-permute-start = (bf16[768,384]{1,0:T(8,128)(2,1)S(1)}, bf16[768,384]{1,0:T(8,128)(2,1)S(1)}, u32[]{:S(2)}, u32[]{:S(2)}) collective-permute-start(bf16[768,384]{1,0:T(8,128)(2,1)S(1)} %constant_dynamic-update-slice_fusion.refs_1_.w00), channel_id=1, source_target_pairs={{0,32},{32,0},{64,96},{96,64},{1,33},{33,1},{65,97},{97,65},{2,34}... | collective-permute-start | bytes 1769480 | tf_op jit(solution)/shard_map/ppermute | solution.py:41
  46.3 8.8 %all-to-all-done = bf16[16,2,8,384]{3,2,1,0:T(8,128)(2,1)S(1)} async-done(((bf16[16,2,8,384]{3,2,1,0:T(8,128)(2,1)}), bf16[16,2,8,384]{3,2,1,0:T(8,128)(2,1)S(1)}, u32[]{:S(2)}, u32[]{:S(2)}) %all-to-all-start) | async-done | bytes 196640 | tf_op jit(solution)/shard_map/all_to_all | solution.py:37
  55.2 16.4 %all_gather.3.refs_0_ = bf16[256,1536]{1,0:T(8,128)(2,1)S(1)} all-gather(bf16[64,1536]{1,0:T(8,128)(2,1)S(1)} %pad_maximum_fusion), channel_id=1, replica_groups={{1,0,2,3},{5,4,6,7},{9,8,10,11},{13,12,14,15},{17,16,18,19},{21,20,22,2..., dimensions={0}, use_global_device_ids=true | all-gather | bytes 983040 | tf_op jit(solution)/shard_map/all_gather | solution.py:187
  71.6 0.0 collective-permute-done.2.refs_4_.w11
  71.6 0.0 collective-permute-done.1.refs_3_.w10
  71.6 0.0 collective-permute-done.refs_2_.w01
  71.6 1.2 shard_map.68
  72.8 19.2 %all_to_all.25.parts = bf16[8,32,1536]{2,1,0:T(8,128)(2,1)S(1)} all-to-all(bf16[8,32,1536]{2,1,0:T(8,128)(2,1)S(1)} %bitcast.21), channel_id=1, replica_groups=mesh['xh'=2,'y'=4,'core'=2,'xl'=2,'zh'=8,'zl'=4] {'xh','y'}, dimensions={0} | all-to-all | bytes 1572864 | tf_op jit(solution)/shard_map/all_to_all | solution.py:30
  92.1 0.2 shard_map.69
  92.3 16.1 %all_to_all.26 = bf16[8,32,1536]{2,1,0:T(8,128)(2,1)S(1)} all-to-all(bf16[8,32,1536]{2,1,0:T(8,128)(2,1)S(1)} %shard_map.69), channel_id=1, replica_groups=mesh['xh'=2,'y'=4,'core'=2,'xl'=2,'zh'=8,'zl'=4] {'xh','y'}, dimensions={0} | all-to-all | bytes 1572864 | tf_op jit(solution)/shard_map/all_to_all | solution.py:30
  108.3 1.4 shard_map.70
  109.8 3.6 %all-to-all-start.3 = ((bf16[4,64,768]{2,1,0:T(8,128)(2,1)}), bf16[4,64,768]{2,1,0:T(8,128)(2,1)S(1)}, u32[]{:S(2)}, u32[]{:S(2)}) async-start(bf16[4,64,768]{2,1,0:T(8,128)(2,1)} %shard_map.70), calls=%async_computation.3 | async-start | bytes 786432 | tf_op jit(solution)/shard_map/all_to_all | solution.py:213
  113.4 1.8 %shard_map.72 = (bf16[768,384]{1,0:T(8,128)(2,1)}, bf16[768,384]{1,0:T(8,128)(2,1)}, bf16[768,384]{1,0:T(8,128)(2,1)}) custom-call(bf16[256,1536]{1,0:T(8,128)(2,1)S(1)} %copy-done.1, bf16[256,1536]{1,0:T(8,128)(2,1)S(1)} %bitcast.19), custom_call_target="tpu_custom_call" | custom-call | flops 1000000000 | bytes 1024 | tf_op jit(solution)/shard_map/pallas_call | solution.py:55
  115.2 5.3 %collective-permute-start.3 = (bf16[768,384]{1,0:T(8,128)(2,1)}, bf16[768,384]{1,0:T(8,128)(2,1)S(1)}, u32[]{:S(2)}, u32[]{:S(2)}) collective-permute-start(bf16[768,384]{1,0:T(8,128)(2,1)} %get-tuple-element.12), channel_id=1, source_target_pairs={{0,96},{32,64},{64,32},{96,0},{1,97},{33,65},{65,33},{97,1},{2,98}... | collective-permute-start | bytes 1769480 | tf_op jit(solution)/shard_map/ppermute | solution.py:41
  120.5 3.1 %collective-permute-start.4 = (bf16[768,384]{1,0:T(8,128)(2,1)}, bf16[768,384]{1,0:T(8,128)(2,1)S(1)}, u32[]{:S(2)}, u32[]{:S(2)}) collective-permute-start(bf16[768,384]{1,0:T(8,128)(2,1)} %get-tuple-element.13), channel_id=1, source_target_pairs={{0,32},{32,0},{64,96},{96,64},{1,33},{33,1},{65,97},{97,65},{2,34}... | collective-permute-start | bytes 1769480 | tf_op jit(solution)/shard_map/ppermute | solution.py:41
  123.6 1.9 %collective-permute-start.5 = (bf16[768,384]{1,0:T(8,128)(2,1)}, bf16[768,384]{1,0:T(8,128)(2,1)}, u32[]{:S(2)}, u32[]{:S(2)}) collective-permute-start(bf16[768,384]{1,0:T(8,128)(2,1)} %get-tuple-element.14), channel_id=1, source_target_pairs={{0,64},{32,96},{64,0},{96,32},{1,65},{33,97},{65,1},{97,33},{2,66}... | collective-permute-start | bytes 1769480 | tf_op jit(solution)/shard_map/ppermute | solution.py:41
  125.5 0.0 all-to-all-done.3.terms
  125.5 0.7 shard_map.71
  126.2 21.8 %all-to-all-start.4 = ((bf16[16,8,384]{2,1,0:T(8,128)(2,1)}), bf16[16,8,384]{2,1,0:T(8,128)(2,1)S(1)}, u32[]{:S(2)}, u32[]{:S(2)}) async-start(bf16[16,8,384]{2,1,0:T(8,128)(2,1)} %bitcast.11), calls=%async_computation.4 | async-start | bytes 196608 | tf_op jit(solution)/shard_map/all_to_all | solution.py:37
  148.0 0.0 collective-permute-done.3.came0
  148.0 0.0 collective-permute-done.4.came1
  148.0 0.0 collective-permute-done.5.came2
  148.0 2.4 %shard_map.73 = (f32[384,384]{1,0:T(8,128)}, f32[384,384]{1,0:T(8,128)}) custom-call(bf16[256,1536]{1,0:T(8,128)(2,1)S(1)} %copy-done.1, bf16[256,1536]{1,0:T(8,128)(2,1)S(1)} %bitcast.20, bf16[768,384]{1,0:T(8,128)(2,1)S(1)} %collective-permute-done.3.came0, bf16[768,384]{1,0:T(8,128)(2,1)S(1)} %collective-permute-done.4.came1, ...), custom_call_target="tpu_custom_call" | custom-call | flops 30000001024 | bytes 4194304 | tf_op jit(solution)/shard_map/pallas_call | solution.py:55
  150.4 5.5 %all-to-all-done.4 = bf16[16,8,384]{2,1,0:T(8,128)(2,1)S(1)} async-done(((bf16[16,8,384]{2,1,0:T(8,128)(2,1)}), bf16[16,8,384]{2,1,0:T(8,128)(2,1)S(1)}, u32[]{:S(2)}, u32[]{:S(2)}) %all-to-all-start.4) | async-done | bytes 98336 | tf_op jit(solution)/shard_map/all_to_all | solution.py:37
  156.0 0.6 reduce_sum.12
  (9 shorter events, 0.1 us)
Async XLA Ops:
  0.6 37.0 %copy-start.2 = (bf16[384,384]{1,0:T(8,128)(2,1)S(1)}, bf16[384,384]{1,0:T(8,128)(2,1)}, u32[]{:S(2)}) copy-start(bf16[384,384]{1,0:T(8,128)(2,1)} %param.6) | copy-start | bytes 884740
  2.1 53.0 %all-to-all-start = ((bf16[16,2,8,384]{3,2,1,0:T(8,128)(2,1)}), bf16[16,2,8,384]{3,2,1,0:T(8,128)(2,1)S(1)}, u32[]{:S(2)}, u32[]{:S(2)}) async-start(bf16[16,2,8,384]{3,2,1,0:T(8,128)(2,1)} %bitcast.23), calls=%async_computation | async-start | bytes 393216 | tf_op jit(solution)/shard_map/all_to_all | solution.py:37
  37.7 1.0 copy-start.3
  38.7 32.9 %collective-permute-start.2 = (bf16[768,384]{1,0:T(8,128)(2,1)S(1)}, bf16[768,384]{1,0:T(8,128)(2,1)S(1)}, u32[]{:S(2)}, u32[]{:S(2)}) collective-permute-start(bf16[768,384]{1,0:T(8,128)(2,1)S(1)} %constant_dynamic-update-slice_fusion.refs_1_.w00), channel_id=1, source_target_pairs={{0,96},{32,64},{64,32},{96,0},{1,97},{33,65},{65,33},{97,1},{2,98}... | collective-permute-start | bytes 1769480 | tf_op jit(solution)/shard_map/ppermute | solution.py:41
  42.0 29.6 %collective-permute-start.1 = (bf16[768,384]{1,0:T(8,128)(2,1)S(1)}, bf16[768,384]{1,0:T(8,128)(2,1)S(1)}, u32[]{:S(2)}, u32[]{:S(2)}) collective-permute-start(bf16[768,384]{1,0:T(8,128)(2,1)S(1)} %constant_dynamic-update-slice_fusion.refs_1_.w00), channel_id=1, source_target_pairs={{0,64},{32,96},{64,0},{96,32},{1,65},{33,97},{65,1},{97,33},{2,66}... | collective-permute-start | bytes 1769480 | tf_op jit(solution)/shard_map/ppermute | solution.py:41
  44.1 27.5 %collective-permute-start = (bf16[768,384]{1,0:T(8,128)(2,1)S(1)}, bf16[768,384]{1,0:T(8,128)(2,1)S(1)}, u32[]{:S(2)}, u32[]{:S(2)}) collective-permute-start(bf16[768,384]{1,0:T(8,128)(2,1)S(1)} %constant_dynamic-update-slice_fusion.refs_1_.w00), channel_id=1, source_target_pairs={{0,32},{32,0},{64,96},{96,64},{1,33},{33,1},{65,97},{97,65},{2,34}... | collective-permute-start | bytes 1769480 | tf_op jit(solution)/shard_map/ppermute | solution.py:41
  72.8 19.3 %copy-start = (bf16[256,1536]{1,0:T(8,128)(2,1)}, bf16[256,1536]{1,0:T(8,128)(2,1)S(1)}, u32[]{:S(2)}) copy-start(bf16[256,1536]{1,0:T(8,128)(2,1)S(1)} %get-tuple-element.11.near) | copy-start | bytes 2359300
  109.8 3.6 %copy-start.1 = (bf16[256,1536]{1,0:T(8,128)(2,1)S(1)}, bf16[256,1536]{1,0:T(8,128)(2,1)}, u32[]{:S(2)}) copy-start(bf16[256,1536]{1,0:T(8,128)(2,1)} %copy-done) | copy-start | bytes 2359300
  109.8 15.7 %all-to-all-start.3 = ((bf16[4,64,768]{2,1,0:T(8,128)(2,1)}), bf16[4,64,768]{2,1,0:T(8,128)(2,1)S(1)}, u32[]{:S(2)}, u32[]{:S(2)}) async-start(bf16[4,64,768]{2,1,0:T(8,128)(2,1)} %shard_map.70), calls=%async_computation.3 | async-start | bytes 786432 | tf_op jit(solution)/shard_map/all_to_all | solution.py:213
  115.2 32.8 %collective-permute-start.3 = (bf16[768,384]{1,0:T(8,128)(2,1)}, bf16[768,384]{1,0:T(8,128)(2,1)S(1)}, u32[]{:S(2)}, u32[]{:S(2)}) collective-permute-start(bf16[768,384]{1,0:T(8,128)(2,1)} %get-tuple-element.12), channel_id=1, source_target_pairs={{0,96},{32,64},{64,32},{96,0},{1,97},{33,65},{65,33},{97,1},{2,98}... | collective-permute-start | bytes 1769480 | tf_op jit(solution)/shard_map/ppermute | solution.py:41
  120.5 27.5 %collective-permute-start.4 = (bf16[768,384]{1,0:T(8,128)(2,1)}, bf16[768,384]{1,0:T(8,128)(2,1)S(1)}, u32[]{:S(2)}, u32[]{:S(2)}) collective-permute-start(bf16[768,384]{1,0:T(8,128)(2,1)} %get-tuple-element.13), channel_id=1, source_target_pairs={{0,32},{32,0},{64,96},{96,64},{1,33},{33,1},{65,97},{97,65},{2,34}... | collective-permute-start | bytes 1769480 | tf_op jit(solution)/shard_map/ppermute | solution.py:41
  123.6 24.5 %collective-permute-start.5 = (bf16[768,384]{1,0:T(8,128)(2,1)}, bf16[768,384]{1,0:T(8,128)(2,1)}, u32[]{:S(2)}, u32[]{:S(2)}) collective-permute-start(bf16[768,384]{1,0:T(8,128)(2,1)} %get-tuple-element.14), channel_id=1, source_target_pairs={{0,64},{32,96},{64,0},{96,32},{1,65},{33,97},{65,1},{97,33},{2,66}... | collective-permute-start | bytes 1769480 | tf_op jit(solution)/shard_map/ppermute | solution.py:41
  126.2 29.8 %all-to-all-start.4 = ((bf16[16,8,384]{2,1,0:T(8,128)(2,1)}), bf16[16,8,384]{2,1,0:T(8,128)(2,1)S(1)}, u32[]{:S(2)}, u32[]{:S(2)}) async-start(bf16[16,8,384]{2,1,0:T(8,128)(2,1)} %bitcast.11), calls=%async_computation.4 | async-start | bytes 196608 | tf_op jit(solution)/shard_map/all_to_all | solution.py:37

commit v7 on v6

--- a/solution.py
+++ b/solution.py
@@ -104,12 +104,7 @@
     copy.wait()
 
 
-def forward_kernel(*refs):
-    pieces, (w00, w01, w10, w11, near, parts) = refs[:-6], refs[-6:]
-    at = 0
-    for piece in pieces:
-        near[at : at + piece.shape[0]] = piece[...]
-        at += piece.shape[0]
+def forward_kernel(near, w00, w01, w10, w11, parts):
     width = w00.shape[1]
     for c, (own, other) in enumerate(((w00, w10), (w01, w11))):
         for j in range(2):
@@ -184,14 +179,9 @@
     other_in, other_grad = [jnp.where(core == 0, f[1], f[0]) for f in far]
     far = jnp.concatenate([own_in, other_in, own_grad, other_grad], axis=1)
 
-    pieces = [lax.all_gather(far, RING, axis=0, axis_index_groups=FOLD, tiled=True)]
-    tokens = 32 * half
-    near, parts = call(
-        forward_kernel,
-        [((tokens, 4 * width), BF16), ((tokens, 4 * width), BF16)],
-        *pieces,
-        *held,
-    )
+    near = lax.all_gather(far, RING, axis=0, axis_index_groups=FOLD, tiled=True)
+    tokens = near.shape[0]
+    (parts,) = call(forward_kernel, [((tokens, 4 * width), BF16)], near, *held)
     parts = exchange(parts.reshape(8, tokens // 8, 4 * width), PLANE)
     (both,) = call(act_kernel, [(parts.shape, BF16)], parts, far=1)
     both = exchange(both, PLANE)

time: 157 us -> 157 us (level)
  no operation moved by 1% of the time
where the time goes in v7:
time: 157 us
  starting transfers between devices  78.6 us (50%)
  blocking collectives  51.9 us (33%)
  waiting for transfers between devices  14.4 us (9%)
  Pallas kernels  8.59 us (5%)
  local copies, waits for them, and re-layouts  1.75 us (1%)
    all_to_all x2, starting transfers between devices, exchange_far(): lax.all_to_all(blocks, SPAN, 0, 0, axis_index_groups=groups, tiled=False)  57.3 us
    all_to_all x2, blocking collectives, exchange(): return lax.all_to_all(blocks, axes, 0, 0, tiled=False)  35.4 us
    ppermute x6, starting transfers between devices, flip(): lax.ppermute(block, QUAD, [(i, i ^ 2 * slab + column) for i in range(4)])  17.9 us
    all_gather x1, blocking collectives, local(): near = lax.all_gather(far, RING, axis=0, axis_index_groups=FOLD, tiled=True)  16.4 us
    all_to_all x2, waiting for transfers between devices, exchange_far(): lax.all_to_all(blocks, SPAN, 0, 0, axis_index_groups=groups, tiled=False)  14.4 us
    pallas_call x7, Pallas kernels, call(): pl.pallas_call(kernel, out_shape=[jax.ShapeDtypeStruct(shape, kind) for s...  8.59 us
    all_to_all x1, starting transfers between devices, local(): lax.all_to_all(terms, RING, 0, 0, axis_index_groups=FOLD, tiled=False)  3.45 us
  transfers between devices with their start and end apart: 9, of which 2 were waited for; matrix products, arithmetic and copies ran while one was open for 0% of the time, Pallas kernels for 3%

profile of v7, /device:TPU:1, one launch (start us, length us, event | category | flops | bytes accessed | tf_op | source)
XLA Modules:
  0.0 156.8 jit_solution(7168525806305307438)
XLA Ops:
  0.6 1.5 shard_map.67
  2.1 35.5 %all-to-all-start = ((bf16[16,2,8,384]{3,2,1,0:T(8,128)(2,1)}), bf16[16,2,8,384]{3,2,1,0:T(8,128)(2,1)S(1)}, u32[]{:S(2)}, u32[]{:S(2)}) async-start(bf16[16,2,8,384]{3,2,1,0:T(8,128)(2,1)} %bitcast.23), calls=%async_computation | async-start | bytes 393216 | tf_op jit(solution)/shard_map/all_to_all | solution.py:37
  37.7 0.0 copy-start.4
  37.7 0.9 copy-done.4
  38.7 3.4 %collective-permute-start.2 = (bf16[768,384]{1,0:T(8,128)(2,1)S(1)}, bf16[768,384]{1,0:T(8,128)(2,1)S(1)}, u32[]{:S(2)}, u32[]{:S(2)}) collective-permute-start(bf16[768,384]{1,0:T(8,128)(2,1)S(1)} %constant_dynamic-update-slice_fusion.w00), channel_id=1, source_target_pairs={{0,96},{32,64},{64,32},{96,0},{1,97},{33,65},{65,33},{97,1},{2,98}... | collective-permute-start | bytes 1769480 | tf_op jit(solution)/shard_map/ppermute | solution.py:41
  42.0 2.1 %collective-permute-start.1 = (bf16[768,384]{1,0:T(8,128)(2,1)S(1)}, bf16[768,384]{1,0:T(8,128)(2,1)S(1)}, u32[]{:S(2)}, u32[]{:S(2)}) collective-permute-start(bf16[768,384]{1,0:T(8,128)(2,1)S(1)} %constant_dynamic-update-slice_fusion.w00), channel_id=1, source_target_pairs={{0,64},{32,96},{64,0},{96,32},{1,65},{33,97},{65,1},{97,33},{2,66}... | collective-permute-start | bytes 1769480 | tf_op jit(solution)/shard_map/ppermute | solution.py:41
  44.1 2.2 %collective-permute-start = (bf16[768,384]{1,0:T(8,128)(2,1)S(1)}, bf16[768,384]{1,0:T(8,128)(2,1)S(1)}, u32[]{:S(2)}, u32[]{:S(2)}) collective-permute-start(bf16[768,384]{1,0:T(8,128)(2,1)S(1)} %constant_dynamic-update-slice_fusion.w00), channel_id=1, source_target_pairs={{0,32},{32,0},{64,96},{96,64},{1,33},{33,1},{65,97},{97,65},{2,34}... | collective-permute-start | bytes 1769480 | tf_op jit(solution)/shard_map/ppermute | solution.py:41
  46.3 8.8 %all-to-all-done = bf16[16,2,8,384]{3,2,1,0:T(8,128)(2,1)S(1)} async-done(((bf16[16,2,8,384]{3,2,1,0:T(8,128)(2,1)}), bf16[16,2,8,384]{3,2,1,0:T(8,128)(2,1)S(1)}, u32[]{:S(2)}, u32[]{:S(2)}) %all-to-all-start) | async-done | bytes 196640 | tf_op jit(solution)/shard_map/all_to_all | solution.py:37
  55.2 16.4 %all_gather.3.near = bf16[256,1536]{1,0:T(8,128)(2,1)S(1)} all-gather(bf16[64,1536]{1,0:T(8,128)(2,1)S(1)} %pad_maximum_fusion), channel_id=1, replica_groups={{1,0,2,3},{5,4,6,7},{9,8,10,11},{13,12,14,15},{17,16,18,19},{21,20,22,2..., dimensions={0}, use_global_device_ids=true | all-gather | bytes 983040 | tf_op jit(solution)/shard_map/all_gather | solution.py:182
  71.6 0.0 collective-permute-done.2.w11
  71.6 0.0 collective-permute-done.1.w10
  71.6 0.0 collective-permute-done.w01
  71.6 0.0 copy-start
  71.6 1.1 shard_map.68
  72.8 19.3 %all_to_all.25.parts = bf16[8,32,1536]{2,1,0:T(8,128)(2,1)S(1)} all-to-all(bf16[8,32,1536]{2,1,0:T(8,128)(2,1)S(1)} %bitcast.18), channel_id=1, replica_groups=mesh['xh'=2,'y'=4,'core'=2,'xl'=2,'zh'=8,'zl'=4] {'xh','y'}, dimensions={0} | all-to-all | bytes 1572864 | tf_op jit(solution)/shard_map/all_to_all | solution.py:30
  92.1 0.2 shard_map.69
  92.3 0.0 copy-start.1
  92.3 16.2 %all_to_all.26 = bf16[8,32,1536]{2,1,0:T(8,128)(2,1)S(1)} all-to-all(bf16[8,32,1536]{2,1,0:T(8,128)(2,1)S(1)} %shard_map.69), channel_id=1, replica_groups=mesh['xh'=2,'y'=4,'core'=2,'xl'=2,'zh'=8,'zl'=4] {'xh','y'}, dimensions={0} | all-to-all | bytes 1572864 | tf_op jit(solution)/shard_map/all_to_all | solution.py:30
  108.5 0.9 shard_map.70
  109.4 0.7 copy-done.2
  110.1 3.4 %all-to-all-start.3 = ((bf16[4,64,768]{2,1,0:T(8,128)(2,1)}), bf16[4,64,768]{2,1,0:T(8,128)(2,1)S(1)}, u32[]{:S(2)}, u32[]{:S(2)}) async-start(bf16[4,64,768]{2,1,0:T(8,128)(2,1)} %copy-done.2), calls=%async_computation.3 | async-start | bytes 786432 | tf_op jit(solution)/shard_map/all_to_all | solution.py:203
  113.6 1.8 %shard_map.72 = (bf16[768,384]{1,0:T(8,128)(2,1)}, bf16[768,384]{1,0:T(8,128)(2,1)}, bf16[768,384]{1,0:T(8,128)(2,1)}) custom-call(bf16[256,1536]{1,0:T(8,128)(2,1)S(1)} %all_gather.3.near, bf16[256,1536]{1,0:T(8,128)(2,1)S(1)} %bitcast.20), custom_call_target="tpu_custom_call" | custom-call | flops 1000000000 | bytes 1024 | tf_op jit(solution)/shard_map/pallas_call | solution.py:55
  115.4 5.3 %collective-permute-start.3 = (bf16[768,384]{1,0:T(8,128)(2,1)}, bf16[768,384]{1,0:T(8,128)(2,1)S(1)}, u32[]{:S(2)}, u32[]{:S(2)}) collective-permute-start(bf16[768,384]{1,0:T(8,128)(2,1)} %get-tuple-element.8), channel_id=1, source_target_pairs={{0,96},{32,64},{64,32},{96,0},{1,97},{33,65},{65,33},{97,1},{2,98}... | collective-permute-start | bytes 1769480 | tf_op jit(solution)/shard_map/ppermute | solution.py:41
  120.7 3.1 %collective-permute-start.4 = (bf16[768,384]{1,0:T(8,128)(2,1)}, bf16[768,384]{1,0:T(8,128)(2,1)S(1)}, u32[]{:S(2)}, u32[]{:S(2)}) collective-permute-start(bf16[768,384]{1,0:T(8,128)(2,1)} %get-tuple-element.9), channel_id=1, source_target_pairs={{0,32},{32,0},{64,96},{96,64},{1,33},{33,1},{65,97},{97,65},{2,34}... | collective-permute-start | bytes 1769480 | tf_op jit(solution)/shard_map/ppermute | solution.py:41
  123.7 1.9 %collective-permute-start.5 = (bf16[768,384]{1,0:T(8,128)(2,1)}, bf16[768,384]{1,0:T(8,128)(2,1)}, u32[]{:S(2)}, u32[]{:S(2)}) collective-permute-start(bf16[768,384]{1,0:T(8,128)(2,1)} %get-tuple-element.10), channel_id=1, source_target_pairs={{0,64},{32,96},{64,0},{96,32},{1,65},{33,97},{65,1},{97,33},{2,66}... | collective-permute-start | bytes 1769480 | tf_op jit(solution)/shard_map/ppermute | solution.py:41
  125.7 0.7 shard_map.71
  126.4 21.8 %all-to-all-start.4 = ((bf16[16,8,384]{2,1,0:T(8,128)(2,1)}), bf16[16,8,384]{2,1,0:T(8,128)(2,1)S(1)}, u32[]{:S(2)}, u32[]{:S(2)}) async-start(bf16[16,8,384]{2,1,0:T(8,128)(2,1)} %bitcast.11), calls=%async_computation.4 | async-start | bytes 196608 | tf_op jit(solution)/shard_map/all_to_all | solution.py:37
  148.2 0.0 collective-permute-done.3.came0
  148.2 0.0 collective-permute-done.5.came2
  148.2 2.4 %shard_map.73 = (f32[384,384]{1,0:T(8,128)}, f32[384,384]{1,0:T(8,128)}) custom-call(bf16[256,1536]{1,0:T(8,128)(2,1)S(1)} %all_gather.3.near, bf16[256,1536]{1,0:T(8,128)(2,1)S(1)} %bitcast.21, bf16[768,384]{1,0:T(8,128)(2,1)S(1)} %collective-permute-done.3.came0, bf16[768,384]{1,0:T(8,128)(2,1)S(1)} %collective-permute-done.4.came1, ...), custom_call_target="tpu_custom_call" | custom-call | flops 30000001024 | bytes 4194304 | tf_op jit(solution)/shard_map/pallas_call | solution.py:55
  150.6 5.5 %all-to-all-done.4 = bf16[16,8,384]{2,1,0:T(8,128)(2,1)S(1)} async-done(((bf16[16,8,384]{2,1,0:T(8,128)(2,1)}), bf16[16,8,384]{2,1,0:T(8,128)(2,1)S(1)}, u32[]{:S(2)}, u32[]{:S(2)}) %all-to-all-start.4) | async-done | bytes 98336 | tf_op jit(solution)/shard_map/all_to_all | solution.py:37
  156.1 0.6 reduce_sum.12
  (11 shorter events, 0.1 us)
Async XLA Ops:
  0.6 37.0 %copy-start.3 = (bf16[384,384]{1,0:T(8,128)(2,1)S(1)}, bf16[384,384]{1,0:T(8,128)(2,1)}, u32[]{:S(2)}) copy-start(bf16[384,384]{1,0:T(8,128)(2,1)} %param.6) | copy-start | bytes 884740
  2.1 53.0 %all-to-all-start = ((bf16[16,2,8,384]{3,2,1,0:T(8,128)(2,1)}), bf16[16,2,8,384]{3,2,1,0:T(8,128)(2,1)S(1)}, u32[]{:S(2)}, u32[]{:S(2)}) async-start(bf16[16,2,8,384]{3,2,1,0:T(8,128)(2,1)} %bitcast.23), calls=%async_computation | async-start | bytes 393216 | tf_op jit(solution)/shard_map/all_to_all | solution.py:37
  37.7 1.0 copy-start.4
  38.7 32.9 %collective-permute-start.2 = (bf16[768,384]{1,0:T(8,128)(2,1)S(1)}, bf16[768,384]{1,0:T(8,128)(2,1)S(1)}, u32[]{:S(2)}, u32[]{:S(2)}) collective-permute-start(bf16[768,384]{1,0:T(8,128)(2,1)S(1)} %constant_dynamic-update-slice_fusion.w00), channel_id=1, source_target_pairs={{0,96},{32,64},{64,32},{96,0},{1,97},{33,65},{65,33},{97,1},{2,98}... | collective-permute-start | bytes 1769480 | tf_op jit(solution)/shard_map/ppermute | solution.py:41
  42.0 29.6 %collective-permute-start.1 = (bf16[768,384]{1,0:T(8,128)(2,1)S(1)}, bf16[768,384]{1,0:T(8,128)(2,1)S(1)}, u32[]{:S(2)}, u32[]{:S(2)}) collective-permute-start(bf16[768,384]{1,0:T(8,128)(2,1)S(1)} %constant_dynamic-update-slice_fusion.w00), channel_id=1, source_target_pairs={{0,64},{32,96},{64,0},{96,32},{1,65},{33,97},{65,1},{97,33},{2,66}... | collective-permute-start | bytes 1769480 | tf_op jit(solution)/shard_map/ppermute | solution.py:41
  44.1 27.5 %collective-permute-start = (bf16[768,384]{1,0:T(8,128)(2,1)S(1)}, bf16[768,384]{1,0:T(8,128)(2,1)S(1)}, u32[]{:S(2)}, u32[]{:S(2)}) collective-permute-start(bf16[768,384]{1,0:T(8,128)(2,1)S(1)} %constant_dynamic-update-slice_fusion.w00), channel_id=1, source_target_pairs={{0,32},{32,0},{64,96},{96,64},{1,33},{33,1},{65,97},{97,65},{2,34}... | collective-permute-start | bytes 1769480 | tf_op jit(solution)/shard_map/ppermute | solution.py:41
  71.6 1.2 copy-start
  92.3 16.2 %copy-start.1 = (bf16[768,384]{1,0:T(8,128)(2,1)S(1)}, bf16[768,384]{1,0:T(8,128)(2,1)}, u32[]{:S(2)}) copy-start(bf16[768,384]{1,0:T(8,128)(2,1)} %copy-done) | copy-start | bytes 1769476
  109.4 0.7 copy-start.2
  110.1 15.5 %all-to-all-start.3 = ((bf16[4,64,768]{2,1,0:T(8,128)(2,1)}), bf16[4,64,768]{2,1,0:T(8,128)(2,1)S(1)}, u32[]{:S(2)}, u32[]{:S(2)}) async-start(bf16[4,64,768]{2,1,0:T(8,128)(2,1)} %copy-done.2), calls=%async_computation.3 | async-start | bytes 786432 | tf_op jit(solution)/shard_map/all_to_all | solution.py:203
  115.4 32.8 %collective-permute-start.3 = (bf16[768,384]{1,0:T(8,128)(2,1)}, bf16[768,384]{1,0:T(8,128)(2,1)S(1)}, u32[]{:S(2)}, u32[]{:S(2)}) collective-permute-start(bf16[768,384]{1,0:T(8,128)(2,1)} %get-tuple-element.8), channel_id=1, source_target_pairs={{0,96},{32,64},{64,32},{96,0},{1,97},{33,65},{65,33},{97,1},{2,98}... | collective-permute-start | bytes 1769480 | tf_op jit(solution)/shard_map/ppermute | solution.py:41
  120.7 27.5 %collective-permute-start.4 = (bf16[768,384]{1,0:T(8,128)(2,1)}, bf16[768,384]{1,0:T(8,128)(2,1)S(1)}, u32[]{:S(2)}, u32[]{:S(2)}) collective-permute-start(bf16[768,384]{1,0:T(8,128)(2,1)} %get-tuple-element.9), channel_id=1, source_target_pairs={{0,32},{32,0},{64,96},{96,64},{1,33},{33,1},{65,97},{97,65},{2,34}... | collective-permute-start | bytes 1769480 | tf_op jit(solution)/shard_map/ppermute | solution.py:41
  123.7 24.5 %collective-permute-start.5 = (bf16[768,384]{1,0:T(8,128)(2,1)}, bf16[768,384]{1,0:T(8,128)(2,1)}, u32[]{:S(2)}, u32[]{:S(2)}) collective-permute-start(bf16[768,384]{1,0:T(8,128)(2,1)} %get-tuple-element.10), channel_id=1, source_target_pairs={{0,64},{32,96},{64,0},{96,32},{1,65},{33,97},{65,1},{97,33},{2,66}... | collective-permute-start | bytes 1769480 | tf_op jit(solution)/shard_map/ppermute | solution.py:41
  126.4 29.8 %all-to-all-start.4 = ((bf16[16,8,384]{2,1,0:T(8,128)(2,1)}), bf16[16,8,384]{2,1,0:T(8,128)(2,1)S(1)}, u32[]{:S(2)}, u32[]{:S(2)}) async-start(bf16[16,8,384]{2,1,0:T(8,128)(2,1)} %bitcast.11), calls=%async_computation.4 | async-start | bytes 196608 | tf_op jit(solution)/shard_map/all_to_all | solution.py:37

commit v8 on v7

--- a/solution.py
+++ b/solution.py
@@ -114,7 +114,7 @@
             parts[:, (2 * j + c) * width : (2 * j + c + 1) * width] = sums.astype(BF16)
 
 
-def terms_kernel(core, both, w00, w01, w10, w11, terms, held, done):
+def terms_kernel(core, both, w00, w01, w10, w11, terms):
     width = w00.shape[1]
     d = [both[:, (2 + c) * width : (3 + c) * width] for c in range(2)]
     slabs = [
@@ -123,10 +123,7 @@
     ]
     for a in range(2):
         chosen = jnp.where(core[0] == a, slabs[0], slabs[1]).astype(BF16)
-        held[:, :, a * width : (a + 1) * width] = chosen.reshape(4, 64, width)
-    copy = pltpu.make_async_copy(held, terms, done)
-    copy.start()
-    copy.wait()
+        terms[:, :, a * width : (a + 1) * width] = chosen.reshape(4, 64, width)
 
 
 def two_grads(near, both, slab, column):
@@ -194,7 +191,6 @@
         both,
         *held,
         scalars=1,
-        far=1,
         cost=BOUND,
     )
     blocks = [((2 * width, width), BF16)] * 3

time: 157 us -> 157 us (level)
  no operation moved by 1% of the time
where the time goes in v8:
time: 157 us
  starting transfers between devices  78.6 us (50%)
  blocking collectives  51.9 us (33%)
  waiting for transfers between devices  14.4 us (9%)
  Pallas kernels  8.39 us (5%)
  local copies, waits for them, and re-layouts  1.75 us (1%)
    all_to_all x2, starting transfers between devices, exchange_far(): lax.all_to_all(blocks, SPAN, 0, 0, axis_index_groups=groups, tiled=False)  57.3 us
    all_to_all x2, blocking collectives, exchange(): return lax.all_to_all(blocks, axes, 0, 0, tiled=False)  35.4 us
    ppermute x6, starting transfers between devices, flip(): lax.ppermute(block, QUAD, [(i, i ^ 2 * slab + column) for i in range(4)])  17.9 us
    all_gather x1, blocking collectives, local(): near = lax.all_gather(far, RING, axis=0, axis_index_groups=FOLD, tiled=True)  16.4 us
    all_to_all x2, waiting for transfers between devices, exchange_far(): lax.all_to_all(blocks, SPAN, 0, 0, axis_index_groups=groups, tiled=False)  14.4 us
    pallas_call x7, Pallas kernels, call(): pl.pallas_call(kernel, out_shape=[jax.ShapeDtypeStruct(shape, kind) for s...  8.39 us
    all_to_all x1, starting transfers between devices, local(): lax.all_to_all(terms, RING, 0, 0, axis_index_groups=FOLD, tiled=False)  3.45 us
  transfers between devices with their start and end apart: 9, of which 2 were waited for; matrix products, arithmetic and copies ran while one was open for 0% of the time, Pallas kernels for 3%

profile of v8, /device:TPU:1, one launch (start us, length us, event | category | flops | bytes accessed | tf_op | source)
XLA Modules:
  0.0 156.6 jit_solution(7705834291731472629)
XLA Ops:
  0.6 1.5 shard_map.67
  2.1 35.5 %all-to-all-start = ((bf16[16,2,8,384]{3,2,1,0:T(8,128)(2,1)}), bf16[16,2,8,384]{3,2,1,0:T(8,128)(2,1)S(1)}, u32[]{:S(2)}, u32[]{:S(2)}) async-start(bf16[16,2,8,384]{3,2,1,0:T(8,128)(2,1)} %bitcast.23), calls=%async_computation | async-start | bytes 393216 | tf_op jit(solution)/shard_map/all_to_all | solution.py:37
  37.7 0.0 copy-start.4
  37.7 0.9 copy-done.4
  38.7 3.4 %collective-permute-start.2 = (bf16[768,384]{1,0:T(8,128)(2,1)S(1)}, bf16[768,384]{1,0:T(8,128)(2,1)S(1)}, u32[]{:S(2)}, u32[]{:S(2)}) collective-permute-start(bf16[768,384]{1,0:T(8,128)(2,1)S(1)} %constant_dynamic-update-slice_fusion.w00), channel_id=1, source_target_pairs={{0,96},{32,64},{64,32},{96,0},{1,97},{33,65},{65,33},{97,1},{2,98}... | collective-permute-start | bytes 1769480 | tf_op jit(solution)/shard_map/ppermute | solution.py:41
  42.0 2.1 %collective-permute-start.1 = (bf16[768,384]{1,0:T(8,128)(2,1)S(1)}, bf16[768,384]{1,0:T(8,128)(2,1)S(1)}, u32[]{:S(2)}, u32[]{:S(2)}) collective-permute-start(bf16[768,384]{1,0:T(8,128)(2,1)S(1)} %constant_dynamic-update-slice_fusion.w00), channel_id=1, source_target_pairs={{0,64},{32,96},{64,0},{96,32},{1,65},{33,97},{65,1},{97,33},{2,66}... | collective-permute-start | bytes 1769480 | tf_op jit(solution)/shard_map/ppermute | solution.py:41
  44.1 2.2 %collective-permute-start = (bf16[768,384]{1,0:T(8,128)(2,1)S(1)}, bf16[768,384]{1,0:T(8,128)(2,1)S(1)}, u32[]{:S(2)}, u32[]{:S(2)}) collective-permute-start(bf16[768,384]{1,0:T(8,128)(2,1)S(1)} %constant_dynamic-update-slice_fusion.w00), channel_id=1, source_target_pairs={{0,32},{32,0},{64,96},{96,64},{1,33},{33,1},{65,97},{97,65},{2,34}... | collective-permute-start | bytes 1769480 | tf_op jit(solution)/shard_map/ppermute | solution.py:41
  46.3 8.8 %all-to-all-done = bf16[16,2,8,384]{3,2,1,0:T(8,128)(2,1)S(1)} async-done(((bf16[16,2,8,384]{3,2,1,0:T(8,128)(2,1)}), bf16[16,2,8,384]{3,2,1,0:T(8,128)(2,1)S(1)}, u32[]{:S(2)}, u32[]{:S(2)}) %all-to-all-start) | async-done | bytes 196640 | tf_op jit(solution)/shard_map/all_to_all | solution.py:37
  55.2 16.4 %all_gather.3.near = bf16[256,1536]{1,0:T(8,128)(2,1)S(1)} all-gather(bf16[64,1536]{1,0:T(8,128)(2,1)S(1)} %pad_maximum_fusion), channel_id=1, replica_groups={{1,0,2,3},{5,4,6,7},{9,8,10,11},{13,12,14,15},{17,16,18,19},{21,20,22,2..., dimensions={0}, use_global_device_ids=true | all-gather | bytes 983040 | tf_op jit(solution)/shard_map/all_gather | solution.py:179
  71.6 0.0 collective-permute-done.2.w11
  71.6 0.0 collective-permute-done.1.w10
  71.6 0.0 collective-permute-done.w01
  71.6 0.0 copy-start
  71.6 1.1 shard_map.68
  72.8 19.3 %all_to_all.25.parts = bf16[8,32,1536]{2,1,0:T(8,128)(2,1)S(1)} all-to-all(bf16[8,32,1536]{2,1,0:T(8,128)(2,1)S(1)} %bitcast.18), channel_id=1, replica_groups=mesh['xh'=2,'y'=4,'core'=2,'xl'=2,'zh'=8,'zl'=4] {'xh','y'}, dimensions={0} | all-to-all | bytes 1572864 | tf_op jit(solution)/shard_map/all_to_all | solution.py:30
  92.1 0.2 shard_map.69
  92.3 0.0 copy-start.1
  92.3 16.2 %all_to_all.26 = bf16[8,32,1536]{2,1,0:T(8,128)(2,1)S(1)} all-to-all(bf16[8,32,1536]{2,1,0:T(8,128)(2,1)S(1)} %shard_map.69), channel_id=1, replica_groups=mesh['xh'=2,'y'=4,'core'=2,'xl'=2,'zh'=8,'zl'=4] {'xh','y'}, dimensions={0} | all-to-all | bytes 1572864 | tf_op jit(solution)/shard_map/all_to_all | solution.py:30
  108.5 0.7 shard_map.70
  109.2 0.7 copy-done.2
  109.9 3.4 %all-to-all-start.3 = ((bf16[4,64,768]{2,1,0:T(8,128)(2,1)}), bf16[4,64,768]{2,1,0:T(8,128)(2,1)S(1)}, u32[]{:S(2)}, u32[]{:S(2)}) async-start(bf16[4,64,768]{2,1,0:T(8,128)(2,1)} %copy-done.2), calls=%async_computation.3 | async-start | bytes 786432 | tf_op jit(solution)/shard_map/all_to_all | solution.py:199
  113.4 1.8 %shard_map.72 = (bf16[768,384]{1,0:T(8,128)(2,1)}, bf16[768,384]{1,0:T(8,128)(2,1)}, bf16[768,384]{1,0:T(8,128)(2,1)}) custom-call(bf16[256,1536]{1,0:T(8,128)(2,1)S(1)} %all_gather.3.near, bf16[256,1536]{1,0:T(8,128)(2,1)S(1)} %bitcast.20), custom_call_target="tpu_custom_call" | custom-call | flops 1000000000 | bytes 1024 | tf_op jit(solution)/shard_map/pallas_call | solution.py:55
  115.2 5.3 %collective-permute-start.3 = (bf16[768,384]{1,0:T(8,128)(2,1)}, bf16[768,384]{1,0:T(8,128)(2,1)S(1)}, u32[]{:S(2)}, u32[]{:S(2)}) collective-permute-start(bf16[768,384]{1,0:T(8,128)(2,1)} %get-tuple-element.8), channel_id=1, source_target_pairs={{0,96},{32,64},{64,32},{96,0},{1,97},{33,65},{65,33},{97,1},{2,98}... | collective-permute-start | bytes 1769480 | tf_op jit(solution)/shard_map/ppermute | solution.py:41
  120.5 3.1 %collective-permute-start.4 = (bf16[768,384]{1,0:T(8,128)(2,1)}, bf16[768,384]{1,0:T(8,128)(2,1)S(1)}, u32[]{:S(2)}, u32[]{:S(2)}) collective-permute-start(bf16[768,384]{1,0:T(8,128)(2,1)} %get-tuple-element.9), channel_id=1, source_target_pairs={{0,32},{32,0},{64,96},{96,64},{1,33},{33,1},{65,97},{97,65},{2,34}... | collective-permute-start | bytes 1769480 | tf_op jit(solution)/shard_map/ppermute | solution.py:41
  123.5 1.9 %collective-permute-start.5 = (bf16[768,384]{1,0:T(8,128)(2,1)}, bf16[768,384]{1,0:T(8,128)(2,1)}, u32[]{:S(2)}, u32[]{:S(2)}) collective-permute-start(bf16[768,384]{1,0:T(8,128)(2,1)} %get-tuple-element.10), channel_id=1, source_target_pairs={{0,64},{32,96},{64,0},{96,32},{1,65},{33,97},{65,1},{97,33},{2,66}... | collective-permute-start | bytes 1769480 | tf_op jit(solution)/shard_map/ppermute | solution.py:41
  125.5 0.7 shard_map.71
  126.2 21.8 %all-to-all-start.4 = ((bf16[16,8,384]{2,1,0:T(8,128)(2,1)}), bf16[16,8,384]{2,1,0:T(8,128)(2,1)S(1)}, u32[]{:S(2)}, u32[]{:S(2)}) async-start(bf16[16,8,384]{2,1,0:T(8,128)(2,1)} %bitcast.11), calls=%async_computation.4 | async-start | bytes 196608 | tf_op jit(solution)/shard_map/all_to_all | solution.py:37
  148.0 0.0 collective-permute-done.3.came0
  148.0 0.0 collective-permute-done.5.came2
  148.0 2.4 %shard_map.73 = (f32[384,384]{1,0:T(8,128)}, f32[384,384]{1,0:T(8,128)}) custom-call(bf16[256,1536]{1,0:T(8,128)(2,1)S(1)} %all_gather.3.near, bf16[256,1536]{1,0:T(8,128)(2,1)S(1)} %bitcast.21, bf16[768,384]{1,0:T(8,128)(2,1)S(1)} %collective-permute-done.3.came0, bf16[768,384]{1,0:T(8,128)(2,1)S(1)} %collective-permute-done.4.came1, ...), custom_call_target="tpu_custom_call" | custom-call | flops 30000001024 | bytes 4194304 | tf_op jit(solution)/shard_map/pallas_call | solution.py:55
  150.4 5.5 %all-to-all-done.4 = bf16[16,8,384]{2,1,0:T(8,128)(2,1)S(1)} async-done(((bf16[16,8,384]{2,1,0:T(8,128)(2,1)}), bf16[16,8,384]{2,1,0:T(8,128)(2,1)S(1)}, u32[]{:S(2)}, u32[]{:S(2)}) %all-to-all-start.4) | async-done | bytes 98336 | tf_op jit(solution)/shard_map/all_to_all | solution.py:37
  155.9 0.6 reduce_sum.12
  (11 shorter events, 0.1 us)
Async XLA Ops:
  0.6 37.0 %copy-start.3 = (bf16[384,384]{1,0:T(8,128)(2,1)S(1)}, bf16[384,384]{1,0:T(8,128)(2,1)}, u32[]{:S(2)}) copy-start(bf16[384,384]{1,0:T(8,128)(2,1)} %param.6) | copy-start | bytes 884740
  2.1 53.0 %all-to-all-start = ((bf16[16,2,8,384]{3,2,1,0:T(8,128)(2,1)}), bf16[16,2,8,384]{3,2,1,0:T(8,128)(2,1)S(1)}, u32[]{:S(2)}, u32[]{:S(2)}) async-start(bf16[16,2,8,384]{3,2,1,0:T(8,128)(2,1)} %bitcast.23), calls=%async_computation | async-start | bytes 393216 | tf_op jit(solution)/shard_map/all_to_all | solution.py:37
  37.7 1.0 copy-start.4
  38.7 32.9 %collective-permute-start.2 = (bf16[768,384]{1,0:T(8,128)(2,1)S(1)}, bf16[768,384]{1,0:T(8,128)(2,1)S(1)}, u32[]{:S(2)}, u32[]{:S(2)}) collective-permute-start(bf16[768,384]{1,0:T(8,128)(2,1)S(1)} %constant_dynamic-update-slice_fusion.w00), channel_id=1, source_target_pairs={{0,96},{32,64},{64,32},{96,0},{1,97},{33,65},{65,33},{97,1},{2,98}... | collective-permute-start | bytes 1769480 | tf_op jit(solution)/shard_map/ppermute | solution.py:41
  42.0 29.6 %collective-permute-start.1 = (bf16[768,384]{1,0:T(8,128)(2,1)S(1)}, bf16[768,384]{1,0:T(8,128)(2,1)S(1)}, u32[]{:S(2)}, u32[]{:S(2)}) collective-permute-start(bf16[768,384]{1,0:T(8,128)(2,1)S(1)} %constant_dynamic-update-slice_fusion.w00), channel_id=1, source_target_pairs={{0,64},{32,96},{64,0},{96,32},{1,65},{33,97},{65,1},{97,33},{2,66}... | collective-permute-start | bytes 1769480 | tf_op jit(solution)/shard_map/ppermute | solution.py:41
  44.1 27.5 %collective-permute-start = (bf16[768,384]{1,0:T(8,128)(2,1)S(1)}, bf16[768,384]{1,0:T(8,128)(2,1)S(1)}, u32[]{:S(2)}, u32[]{:S(2)}) collective-permute-start(bf16[768,384]{1,0:T(8,128)(2,1)S(1)} %constant_dynamic-update-slice_fusion.w00), channel_id=1, source_target_pairs={{0,32},{32,0},{64,96},{96,64},{1,33},{33,1},{65,97},{97,65},{2,34}... | collective-permute-start | bytes 1769480 | tf_op jit(solution)/shard_map/ppermute | solution.py:41
  71.6 1.2 copy-start
  92.3 16.2 %copy-start.1 = (bf16[768,384]{1,0:T(8,128)(2,1)S(1)}, bf16[768,384]{1,0:T(8,128)(2,1)}, u32[]{:S(2)}) copy-start(bf16[768,384]{1,0:T(8,128)(2,1)} %copy-done) | copy-start | bytes 1769476
  109.2 0.7 copy-start.2
  109.9 15.5 %all-to-all-start.3 = ((bf16[4,64,768]{2,1,0:T(8,128)(2,1)}), bf16[4,64,768]{2,1,0:T(8,128)(2,1)S(1)}, u32[]{:S(2)}, u32[]{:S(2)}) async-start(bf16[4,64,768]{2,1,0:T(8,128)(2,1)} %copy-done.2), calls=%async_computation.3 | async-start | bytes 786432 | tf_op jit(solution)/shard_map/all_to_all | solution.py:199
  115.2 32.8 %collective-permute-start.3 = (bf16[768,384]{1,0:T(8,128)(2,1)}, bf16[768,384]{1,0:T(8,128)(2,1)S(1)}, u32[]{:S(2)}, u32[]{:S(2)}) collective-permute-start(bf16[768,384]{1,0:T(8,128)(2,1)} %get-tuple-element.8), channel_id=1, source_target_pairs={{0,96},{32,64},{64,32},{96,0},{1,97},{33,65},{65,33},{97,1},{2,98}... | collective-permute-start | bytes 1769480 | tf_op jit(solution)/shard_map/ppermute | solution.py:41
  120.5 27.5 %collective-permute-start.4 = (bf16[768,384]{1,0:T(8,128)(2,1)}, bf16[768,384]{1,0:T(8,128)(2,1)S(1)}, u32[]{:S(2)}, u32[]{:S(2)}) collective-permute-start(bf16[768,384]{1,0:T(8,128)(2,1)} %get-tuple-element.9), channel_id=1, source_target_pairs={{0,32},{32,0},{64,96},{96,64},{1,33},{33,1},{65,97},{97,65},{2,34}... | collective-permute-start | bytes 1769480 | tf_op jit(solution)/shard_map/ppermute | solution.py:41
  123.5 24.5 %collective-permute-start.5 = (bf16[768,384]{1,0:T(8,128)(2,1)}, bf16[768,384]{1,0:T(8,128)(2,1)}, u32[]{:S(2)}, u32[]{:S(2)}) collective-permute-start(bf16[768,384]{1,0:T(8,128)(2,1)} %get-tuple-element.10), channel_id=1, source_target_pairs={{0,64},{32,96},{64,0},{96,32},{1,65},{33,97},{65,1},{97,33},{2,66}... | collective-permute-start | bytes 1769480 | tf_op jit(solution)/shard_map/ppermute | solution.py:41
  126.2 29.8 %all-to-all-start.4 = ((bf16[16,8,384]{2,1,0:T(8,128)(2,1)}), bf16[16,8,384]{2,1,0:T(8,128)(2,1)S(1)}, u32[]{:S(2)}, u32[]{:S(2)}) async-start(bf16[16,8,384]{2,1,0:T(8,128)(2,1)} %bitcast.11), calls=%async_computation.4 | async-start | bytes 196608 | tf_op jit(solution)/shard_map/all_to_all | solution.py:37
